TPU v7x, 32 devices: a whole 2x2x4 slice. The times are simulated.
32 devices in a mesh: parts: 2 (over y), rung: 2 (over x), ty: 4 (over z), tx: 2 (over core).
Axes of the slice: x: 2, y: 2, z: 4, core: 2. Of those that a mesh axis runs over, the one named last changes fastest.
Arguments:
- potential: float32 [64, 32, 256], P('parts', 'ty', 'tx'), parts along dimension 0, may hold values from 0 to 3
- labels: int32 [64, 32, 256], P('parts', 'ty', 'tx'), parts along dimension 0, may hold values 0 or 1
- rung_mu: int32 [4], P(('parts', 'rung')), parts along dimension 0, may hold values from 0 to 7
- mu_table: float32 [8], replicated, may hold values from -8.5 to -6.5
- target_table: float32 [8], replicated, may hold values from 0.5 to 1
Outputs:
- potential_grad: float32 [64, 32, 256], P('parts', 'ty', 'tx'), parts along dimension 0
There are 2 independent parts, one for each index of `parts`. A program takes and returns all parts, laid end to end along the dimension named above; an argument that names none is the same for every part. Nothing has to cross between parts.
All inputs are finite; a program needn't handle non-finite values. No bound on the sum of `labels` on one device may be relied on, other than what follows from the above.
Results may differ from a plain program's by a relative error of at most 0.0003.
Values sent between devices are 32-bit elements; how exact they have to be, the bound alone decides.
A program may use at most 64 MiB of HBM per device.

v0:
```python
import math

import jax
import jax.numpy as jnp
from jax import lax
from jax.sharding import PartitionSpec as P

RADIUS = 4


def with_halo(cells, sides, width):
    for axis, dim in sides:
        count = lax.axis_size(axis)
        head = lax.slice_in_dim(cells, 0, width, axis=dim)
        tail = lax.slice_in_dim(cells, cells.shape[dim] - width, cells.shape[dim], axis=dim)
        cells = jnp.concatenate(
            [
                lax.ppermute(tail, axis, [(i, (i + 1) % count) for i in range(count)]),
                cells,
                lax.ppermute(head, axis, [((i + 1) % count, i) for i in range(count)]),
            ],
            axis=dim,
        )
    return cells


def reach_of(allowed, factor, radius):
    height = -1
    for candidate in range(radius + 1):
        if factor * candidate * candidate <= allowed:
            height = candidate
    return height


def span_count(height):
    return 2 * height + 1 if height >= 0 else 0


def stencil_tables(radius):
    entries = []
    shell_count = 0
    for plane_off in range(-radius, radius + 1):
        for row_off in range(-radius, radius + 1):
            square = plane_off * plane_off + row_off * row_off
            ball_reach = reach_of(radius * radius - square, 1, radius)
            inner_reach = reach_of((2 * radius - 1) ** 2 - 4 * square, 4, radius)
            outer_reach = reach_of((2 * radius + 1) ** 2 - 4 * square, 4, radius)
            shell_count += span_count(outer_reach) - span_count(inner_reach)
            if ball_reach >= 0 or outer_reach > inner_reach:
                entries.append((plane_off, row_off, ball_reach, inner_reach, outer_reach))
    return (entries, shell_count)


def box_sums(source, moments):
    span_width = source.shape[-1] - 2 * RADIUS
    center = source[..., RADIUS : RADIUS + span_width]
    box_list = [center]
    moment_list = [jnp.zeros_like(center)]
    for height in range(1, RADIUS + 1):
        right_part = source[..., RADIUS + height : RADIUS + height + span_width]
        left_part = source[..., RADIUS - height : RADIUS - height + span_width]
        box_list.append(box_list[-1] + right_part + left_part)
        if moments:
            moment_list.append(moment_list[-1] + height * (right_part - left_part))
    return (box_list, moment_list)


def window(source, plane_off, row_off):
    planes = source.shape[-3] - 2 * RADIUS
    row_count = source.shape[-2] - 2 * RADIUS
    plane_start = RADIUS + plane_off
    row_start = RADIUS + row_off
    return source[..., plane_start : plane_start + planes, row_start : row_start + row_count, :]


def shell_of(source_list, inner_reach, outer_reach):
    if inner_reach >= 0:
        return source_list[outer_reach] - source_list[inner_reach]
    return source_list[outer_reach]


def spread(grid_field):
    entries, shell_count = stencil_tables(RADIUS)
    area_scale = 4.0 * math.pi * RADIUS * RADIUS / shell_count
    box_list, moment_list = box_sums(grid_field, True)
    volume = jnp.zeros_like(window(box_list[0], 0, 0))
    surface = jnp.zeros_like(volume)
    along_plane = jnp.zeros_like(volume)
    along_row = jnp.zeros_like(volume)
    along_col = jnp.zeros_like(volume)
    for stencil_row in entries:
        plane_off, row_off, ball_reach, inner_reach, outer_reach = stencil_row
        if ball_reach >= 0:
            volume = volume + window(box_list[ball_reach], plane_off, row_off)
        shell_part = window(shell_of(box_list, inner_reach, outer_reach), plane_off, row_off)
        surface = surface + shell_part
        along_plane = along_plane + plane_off * shell_part
        along_row = along_row + row_off * shell_part
        along_col = along_col + window(
            shell_of(moment_list, inner_reach, outer_reach), plane_off, row_off
        )
    vector_scale = area_scale / RADIUS
    return (
        volume,
        area_scale * surface,
        vector_scale * along_plane,
        vector_scale * along_row,
        vector_scale * along_col,
    )


def collect(fields):
    entries, shell_count = stencil_tables(RADIUS)
    area_scale = 4.0 * math.pi * RADIUS * RADIUS / shell_count
    box_list, unused_list = box_sums(fields[0:4], False)
    unused_boxes, moment_list = box_sums(fields[4], True)
    total = jnp.zeros_like(window(box_list[0][0], 0, 0))
    vector_scale = area_scale / RADIUS
    for stencil_row in entries:
        plane_off, row_off, ball_reach, inner_reach, outer_reach = stencil_row
        if ball_reach >= 0:
            total = total + window(box_list[ball_reach][0], plane_off, row_off)
        shell_part = window(shell_of(box_list, inner_reach, outer_reach), plane_off, row_off)
        shell_moment = window(shell_of(moment_list, inner_reach, outer_reach), plane_off, row_off)
        total = (
            total
            + area_scale * shell_part[1]
            - vector_scale * (plane_off * shell_part[2] + row_off * shell_part[3] + shell_moment)
        )
    return total


def energy(volume, surface, vec_plane, vec_row, vec_col):
    free_volume = 1.0 - volume
    vector_sq = vec_plane * vec_plane + vec_row * vec_row + vec_col * vec_col
    first_term = -surface / (4.0 * math.pi * RADIUS * RADIUS) * jnp.log(free_volume)
    second_term = (surface * surface - vector_sq) / (4.0 * math.pi * RADIUS * free_volume)
    third_term = (surface * surface * surface - 3.0 * surface * vector_sq) / (
        24.0 * math.pi * free_volume * free_volume
    )
    return first_term + second_term + third_term


def total_energy(densities):
    return jnp.sum(energy(*densities))


def derivatives(densities):
    return jax.grad(total_energy)(densities)


def hess_apply(densities, vector):
    return jax.vjp(derivatives, densities)[1](vector)[0]


def lookup(table_vals, chosen):
    return jnp.sum(jnp.where(jnp.arange(table_vals.shape[0]) == chosen, table_vals, 0.0))


def pad_planes(grid_field):
    leading = [(0, 0)] * (grid_field.ndim - 3)
    return jnp.pad(grid_field, leading + [(RADIUS, RADIUS), (0, 0), (0, 0)])


def body(potential, labels, rung_mu, mu_table, target_table):
    pore_mask = labels.astype(jnp.float32)
    rung_index = rung_mu[0]
    chem_pot = lookup(mu_table, rung_index)
    target = lookup(target_table, rung_index)
    rho_start = pore_mask * jnp.exp(chem_pot - potential)
    extended = with_halo(rho_start, (("ty", 1), ("tx", 2)), RADIUS)
    densities = spread(pad_planes(extended))
    derivs = derivatives(densities)
    derivs_wide = with_halo(jnp.stack(derivs), (("ty", 2), ("tx", 3)), RADIUS)
    correlation = -collect(pad_planes(derivs_wide))
    weight = pore_mask * jnp.exp(correlation - potential)
    cell_total = weight.size * lax.axis_size("ty") * lax.axis_size("tx")
    amount = lax.psum(jnp.sum(weight), ("ty", "tx")) / cell_total
    coefficient = jnp.log(amount / target) / amount
    weight_wide = with_halo(weight, (("ty", 1), ("tx", 2)), RADIUS)
    images = spread(pad_planes(weight_wide))
    adjoints = hess_apply(densities, images)
    adjoints_wide = with_halo(jnp.stack(adjoints), (("ty", 2), ("tx", 3)), RADIUS)
    pulled_back = collect(pad_planes(adjoints_wide))
    partial_grad = coefficient * (rho_start * pulled_back - weight)
    return lax.psum(partial_grad, "rung")


def solution(mesh):
    return jax.shard_map(
        body,
        mesh=mesh,
        in_specs=(P("parts", "ty", "tx"), P("parts", "ty", "tx"), P(("parts", "rung")), P(), P()),
        out_specs=P("parts", "ty", "tx"),
        check_vma=False,
    )
```

profile of v0, /device:TPU:0, one launch (start us, length us, event | category | flops | bytes accessed | tf_op | source)
XLA Modules:
  0.0 242.7 jit_solution(15759517484644342925)
XLA Ops:
  10.1 3.1 %collective-permute-start = (f32[32,4,128]{2,1,0:T(4,128)S(1)}, f32[32,4,128]{2,1,0:T(4,128)S(1)}, u32[]{:S(2)}, u32[]{:S(2)}) collective-permute-start(f32[32,4,128]{2,1,0:T(4,128)S(1)} %get-tuple-element.95), channel_id=1, source_target_pairs={{0,2},{2,4},{4,6},{6,0},{1,3},{3,5},{5,7},{7,1},{8,10},{10,12},{12... | collective-permute-start | bytes 196616 | tf_op jit(solution)/shard_map/ppermute | solution.py:18
  13.2 2.1 collective-permute-start.1
  15.3 2.3 collective-permute-done
  23.0 3.0 %fusion.29 = (f32[5,32,8,128]{3,2,1,0:T(8,128)S(1)}, f32[32,8,128]{2,1,0:T(8,128)S(1)}, f32[32,8,128]{2,1,0:T(8,128)S(1)}, f32[32,8,128]{2,1,0:T(8,128)S(1)}, f3...) fusion(f32[40,16,136]{2,1,0:T(8,128)S(1)} %select_maximum_fusion.8, f32[40,16,128]{2,1,0:T(8,128)S(1)} %get-tuple-element.52, ...), kind=kLoop, calls=%fused_computation.124 | loop fusion | flops 13008895 | bytes 16384000
  29.5 2.9 %collective-permute-start.5 = (f32[5,32,4,128]{3,1,2,0:T(8,128)}, f32[5,32,4,128]{3,1,2,0:T(8,128)}, u32[]{:S(2)}, u32[]{:S(2)}) collective-permute-start(f32[5,32,4,128]{3,1,2,0:T(8,128)} %copy.55), channel_id=1, source_target_pairs={{2,0},{4,2},{6,4},{0,6},{3,1},{5,3},{7,5},{1,7},{10,8},{12,10},{14... | collective-permute-start | bytes 983048 | tf_op jit(solution)/shard_map/ppermute | solution.py:20
  33.7 6.6 %collective-permute-done.4 = f32[5,32,4,128]{3,1,2,0:T(8,128)} collective-permute-done((f32[5,32,4,128]{3,1,2,0:T(8,128)}, f32[5,32,4,128]{3,1,2,0:T(8,128)}, u32[]{:S(2)}, u32[]{:S(2)}) %collective-permute-start.4) | collective-permute-done | bytes 327712 | tf_op jit(solution)/shard_map/ppermute | solution.py:18
  40.3 2.5 %copy.40 = f32[5,32,4,128]{1,2,3,0:T(4,128)} copy(f32[5,32,4,128]{3,1,2,0:T(8,128)} %collective-permute-done.4) | data formatting | bytes 655360 | tf_op jit(solution)/shard_map/ppermute | solution.py:18
  42.7 3.7 %collective-permute-done.5 = f32[5,32,4,128]{3,1,2,0:T(8,128)} collective-permute-done((f32[5,32,4,128]{3,1,2,0:T(8,128)}, f32[5,32,4,128]{3,1,2,0:T(8,128)}, u32[]{:S(2)}, u32[]{:S(2)}) %collective-permute-start.5) | collective-permute-done | bytes 327712 | tf_op jit(solution)/shard_map/ppermute | solution.py:20
  46.4 2.4 %copy.42 = f32[5,32,4,128]{1,2,3,0:T(4,128)} copy(f32[5,32,4,128]{3,1,2,0:T(8,128)} %collective-permute-done.5) | data formatting | bytes 655360 | tf_op jit(solution)/shard_map/ppermute | solution.py:20
  48.9 2.9 %pad_maximum_fusion = f32[5,32,16,128]{1,2,3,0:T(8,128)S(1)} fusion(f32[5,32,4,128]{1,2,3,0:T(4,128)} %copy.42, f32[5,32,8,128]{1,2,3,0:T(8,128)S(1)} %copy.41, f32[5,32,4,128]{1,2,3,0:T(4,128)} %copy.40), kind=kLoop, calls=%fused_computation | loop fusion | flops 655360 | bytes 2621440 | tf_op jit(solution)/shard_map/concatenate | solution.py:16
  51.8 2.3 copy-done.9
  55.4 5.4 %copy.44 = f32[5,32,16,128]{3,2,1,0:T(8,128)} copy(f32[5,32,16,128]{1,2,3,0:T(8,128)} %copy-done.9) | data formatting | bytes 2621440 | tf_op jit(solution)/shard_map/concatenate | solution.py:16
  64.1 3.2 %select_maximum_fusion.2 = f32[5,40,16,136]{3,2,1,0:T(8,128)S(1)} fusion(f32[5,32,16,4]{3,2,1,0:T(8,128)} %copy.45, f32[5,32,16,128]{3,2,1,0:T(8,128)} %copy.44, f32[5,32,16,4]{3,2,1,0:T(8,128)} %copy.43), kind=kLoop, calls=%fused_computation.6 | loop fusion | flops 3481600 | bytes 3133440 | tf_op jit(solution)/shard_map/concatenate | solution.py:16
  67.3 5.4 %fusion.898 = (f32[4,40,16,128]{3,2,1,0:T(8,128)}, f32[4,40,16,128]{3,2,1,0:T(8,128)}, f32[4,40,16,128]{3,2,1,0:T(8,128)}, f32[4,40,16,128]{3,2,1,0:T(8,128)}, f32[4,40,16,128]{3,2,1,0:T(8,128)}) fusion(f32[5,40,16,136]{3,2,1,0:T(8,128)S(1)} %select_maximum_fusion.2), kind=kLoop, calls=%fused_computation.1844 | loop fusion | flops 2949120 | bytes 18350080 | tf_op jit(solution)/shard_map/sub | solution.py:78
  80.7 2.9 %fusion.713 = f32[32,8,128]{2,1,0:T(8,128)} fusion(f32[4,40,16,128]{3,2,1,0:T(8,128)S(1)} %get-tuple-element.66, f32[40,16,128]{2,1,0:T(8,128)S(1)} %slice_bitcast_fusion.9, f32[40,16,128]{2,1,0:T(8,128)S(1)} %get-tuple-element.73, f32[4,40,16,128]{3,2,1,0:T(8,128)S(1)} %get-tuple-element.65, f32[40,16,128]{2,1,0:T(8,128)S(1)} %slice_bitcast_fusion.8, ...), kind=kLoop, calls=%fused_computation.1395 | loop fusion | flops 7667712 | bytes 17039360 | tf_op jit(solution)/shard_map/add | solution.py:126
  90.3 16.2 %fusion.476 = f32[32,8,128]{2,1,0:T(8,128)S(1)} fusion(f32[32,8,128]{2,1,0:T(8,128)} %convert_element_type.9, f32[32,8,128]{2,1,0:T(8,128)} %param.5, f32[1,32,8,128]{3,2,1,0:T(8,128)} %broadcast.506, f32[1,32,8,128]{3,2,1,0:T(8,128)} %broadcast.509, f32[5,40,16,136]{3,2,1,0:T(8,128)S(1)} %select_maximum_fusion.2, f32[1,32,8,128]{3,2,1,0:T(8,128)} %broadcast.512, ...), kind=kLoop, calls=%fused_computation.982 | loop fusion | flops 11042816 | bytes 26607616 | tf_op jit(solution)/shard_map/mul | solution.py:176
  107.2 3.3 %collective-permute-start.9 = (f32[32,4,128]{2,1,0:T(4,128)S(1)}, f32[32,4,128]{2,1,0:T(4,128)S(1)}, u32[]{:S(2)}, u32[]{:S(2)}) collective-permute-start(f32[32,4,128]{2,1,0:T(4,128)S(1)} %get-tuple-element.94), channel_id=1, source_target_pairs={{2,0},{4,2},{6,4},{0,6},{3,1},{5,3},{7,5},{1,7},{10,8},{12,10},{14... | collective-permute-start | bytes 196616 | tf_op jit(solution)/shard_map/ppermute | solution.py:20
  110.6 2.4 collective-permute-done.8
  118.9 3.1 %fusion.38 = (f32[5,32,8,128]{3,2,1,0:T(8,128)S(1)}, f32[32,8,128]{2,1,0:T(8,128)S(1)}, f32[32,8,128]{2,1,0:T(8,128)S(1)}, f32[32,8,128]{2,1,0:T(8,128)S(1)}, f3...) fusion(f32[32,8,128]{2,1,0:T(8,128)S(1)} %copy-done.31, f32[32,8,128]{2,1,0:T(8,128)S(1)} %copy-done.47, ...), kind=kLoop, calls=%fused_computation.133 | loop fusion | flops 14647295 | bytes 17170432
  130.0 6.1 %collective-permute-done.12 = f32[5,32,4,128]{3,1,2,0:T(8,128)} collective-permute-done((f32[5,32,4,128]{3,1,2,0:T(8,128)}, f32[5,32,4,128]{3,1,2,0:T(8,128)}, u32[]{:S(2)}, u32[]{:S(2)}) %collective-permute-start.12) | collective-permute-done | bytes 327712 | tf_op jit(solution)/shard_map/ppermute | solution.py:18
  136.1 2.5 %copy.48 = f32[5,32,4,128]{1,2,3,0:T(4,128)} copy(f32[5,32,4,128]{3,1,2,0:T(8,128)} %collective-permute-done.12) | data formatting | bytes 655360 | tf_op jit(solution)/shard_map/ppermute | solution.py:18
  138.6 3.9 %collective-permute-done.13 = f32[5,32,4,128]{3,1,2,0:T(8,128)} collective-permute-done((f32[5,32,4,128]{3,1,2,0:T(8,128)}, f32[5,32,4,128]{3,1,2,0:T(8,128)}, u32[]{:S(2)}, u32[]{:S(2)}) %collective-permute-start.13) | collective-permute-done | bytes 327712 | tf_op jit(solution)/shard_map/ppermute | solution.py:20
  142.4 2.4 %copy.50 = f32[5,32,4,128]{1,2,3,0:T(4,128)} copy(f32[5,32,4,128]{3,1,2,0:T(8,128)} %collective-permute-done.13) | data formatting | bytes 655360 | tf_op jit(solution)/shard_map/ppermute | solution.py:20
  144.9 2.9 %pad_maximum_fusion.1 = f32[5,32,16,128]{1,2,3,0:T(8,128)S(1)} fusion(f32[5,32,4,128]{1,2,3,0:T(4,128)} %copy.50, f32[5,32,8,128]{1,2,3,0:T(8,128)S(1)} %copy.49, f32[5,32,4,128]{1,2,3,0:T(4,128)} %copy.48), kind=kLoop, calls=%fused_computation.1 | loop fusion | flops 655360 | bytes 2621440 | tf_op jit(solution)/shard_map/concatenate | solution.py:16
  147.8 2.3 copy-done.8
  151.4 15.9 %psum.14 = f32[]{:T(128)} all-reduce(f32[]{:T(128)} %reduce_sum.28), channel_id=1, replica_groups=mesh['parts'=2,'rung'=2,'ty'=4,'tx'=2] {'ty','tx'}, use_global_device_ids=true, to_apply=%region_2.3 | all-reduce | flops 1 | bytes 8 | tf_op jit(solution)/shard_map/psum | solution.py:178
  168.7 5.4 %copy.52 = f32[5,32,16,128]{3,2,1,0:T(8,128)} copy(f32[5,32,16,128]{1,2,3,0:T(8,128)} %copy-done.8) | data formatting | bytes 2621440 | tf_op jit(solution)/shard_map/concatenate | solution.py:16
  177.4 3.2 %select_maximum_fusion = f32[5,40,16,136]{3,2,1,0:T(8,128)S(1)} fusion(f32[5,32,16,4]{3,2,1,0:T(8,128)} %copy.53, f32[5,32,16,128]{3,2,1,0:T(8,128)} %copy.52, f32[5,32,16,4]{3,2,1,0:T(8,128)} %copy.51), kind=kLoop, calls=%fused_computation.4 | loop fusion | flops 3481600 | bytes 3133440 | tf_op jit(solution)/shard_map/concatenate | solution.py:16
  180.6 5.4 %fusion.893 = (f32[4,40,16,128]{3,2,1,0:T(8,128)}, f32[4,40,16,128]{3,2,1,0:T(8,128)}, f32[4,40,16,128]{3,2,1,0:T(8,128)}, f32[4,40,16,128]{3,2,1,0:T(8,128)}, f32[4,40,16,128]{3,2,1,0:T(8,128)}) fusion(f32[5,40,16,136]{3,2,1,0:T(8,128)S(1)} %select_maximum_fusion), kind=kLoop, calls=%fused_computation.1842 | loop fusion | flops 2949120 | bytes 18350080 | tf_op jit(solution)/shard_map/sub | solution.py:78
  194.0 2.9 %fusion.304 = f32[32,8,128]{2,1,0:T(8,128)} fusion(f32[4,40,16,128]{3,2,1,0:T(8,128)S(1)} %get-tuple-element.63, f32[40,16,128]{2,1,0:T(8,128)S(1)} %slice_bitcast_fusion.4, f32[40,16,128]{2,1,0:T(8,128)S(1)} %get-tuple-element.68, f32[4,40,16,128]{3,2,1,0:T(8,128)S(1)} %get-tuple-element.62, f32[40,16,128]{2,1,0:T(8,128)S(1)} %slice_bitcast_fusion.3, ...), kind=kLoop, calls=%fused_computation.576 | loop fusion | flops 7667712 | bytes 17039360 | tf_op jit(solution)/shard_map/add | solution.py:126
  197.7 16.2 %fusion.67 = f32[32,8,128]{2,1,0:T(8,128)} fusion(f32[32,8,128]{2,1,0:T(8,128)} %mul.3736, f32[32,8,128]{2,1,0:T(8,128)S(1)} %fusion.476, f32[32,8,128]{2,1,0:T(8,128)S(1)} %copy-done.33, f32[1,32,8,128]{3,2,1,0:T(8,128)} %broadcast.506, f32[1,32,8,128]{3,2,1,0:T(8,128)} %broadcast.509, f32[5,40,16,136]{3,2,1,0:T(8,128)S(1)} %select_maximum_fusion, ...), kind=kLoop, calls=%fused_computation.163 | loop fusion | flops 10944512 | bytes 26607616 | tf_op jit(solution)/shard_map/mul | solution.py:185
  213.9 20.0 %all-reduce.6.cloned.1.call-done = f32[32,8,128]{2,1,0:T(8,128)} async-done(((f32[32,8,128]{2,1,0:T(8,128)}), f32[32,8,128]{2,1,0:T(8,128)}) %all-reduce.6.cloned.1.call-update) | async-done | bytes 131088 | tf_op jit(solution)/shard_map/psum | solution.py:186
  (202 shorter events, 61.1 us)
Async XLA Ops:
  6.5 227.4 %all-reduce.6.cloned.1.call-start = ((), (), s32[]{:S(2)}) async-start(), calls=%async_computation | async-start | bytes 262144 | tf_op jit(solution)/shard_map/psum | solution.py:186
  10.1 12.9 %copy-start.32 = (f32[32,8,128]{2,1,0:T(8,128)}, f32[32,8,128]{2,1,0:T(8,128)S(1)}, u32[]{:S(2)}) copy-start(f32[32,8,128]{2,1,0:T(8,128)S(1)} %exponential_multiply_fusion) | copy-start | bytes 393220
  10.1 7.5 %collective-permute-start = (f32[32,4,128]{2,1,0:T(4,128)S(1)}, f32[32,4,128]{2,1,0:T(4,128)S(1)}, u32[]{:S(2)}, u32[]{:S(2)}) collective-permute-start(f32[32,4,128]{2,1,0:T(4,128)S(1)} %get-tuple-element.95), channel_id=1, source_target_pairs={{0,2},{2,4},{4,6},{6,0},{1,3},{3,5},{5,7},{7,1},{8,10},{10,12},{12... | collective-permute-start | bytes 196616 | tf_op jit(solution)/shard_map/ppermute | solution.py:18
  13.2 5.0 %collective-permute-start.1 = (f32[32,4,128]{2,1,0:T(4,128)S(1)}, f32[32,4,128]{2,1,0:T(4,128)S(1)}, u32[]{:S(2)}, u32[]{:S(2)}) collective-permute-start(f32[32,4,128]{2,1,0:T(4,128)S(1)} %get-tuple-element.96), channel_id=1, source_target_pairs={{2,0},{4,2},{6,4},{0,6},{3,1},{5,3},{7,5},{1,7},{10,8},{12,10},{14... | collective-permute-start | bytes 196616 | tf_op jit(solution)/shard_map/ppermute | solution.py:20
  18.4 1.6 collective-permute-start.2
  18.4 1.9 collective-permute-start.3
  27.6 12.7 %collective-permute-start.4 = (f32[5,32,4,128]{3,1,2,0:T(8,128)}, f32[5,32,4,128]{3,1,2,0:T(8,128)}, u32[]{:S(2)}, u32[]{:S(2)}) collective-permute-start(f32[5,32,4,128]{3,1,2,0:T(8,128)} %copy.54), channel_id=1, source_target_pairs={{0,2},{2,4},{4,6},{6,0},{1,3},{3,5},{5,7},{7,1},{8,10},{10,12},{12... | collective-permute-start | bytes 983048 | tf_op jit(solution)/shard_map/ppermute | solution.py:18
  29.5 17.0 %collective-permute-start.5 = (f32[5,32,4,128]{3,1,2,0:T(8,128)}, f32[5,32,4,128]{3,1,2,0:T(8,128)}, u32[]{:S(2)}, u32[]{:S(2)}) collective-permute-start(f32[5,32,4,128]{3,1,2,0:T(8,128)} %copy.55), channel_id=1, source_target_pairs={{2,0},{4,2},{6,4},{0,6},{3,1},{5,3},{7,5},{1,7},{10,8},{12,10},{14... | collective-permute-start | bytes 983048 | tf_op jit(solution)/shard_map/ppermute | solution.py:20
  48.9 5.9 %copy-start.50 = (s32[32,8,128]{2,1,0:T(8,128)S(1)}, s32[32,8,128]{2,1,0:T(8,128)}, u32[]{:S(2)}) copy-start(s32[32,8,128]{2,1,0:T(8,128)} %param.6) | copy-start | bytes 393220
  54.2 6.6 %collective-permute-start.6 = (f32[5,32,16,4]{1,2,3,0:T(8,128)S(1)}, f32[5,32,16,4]{1,2,3,0:T(8,128)S(1)}, u32[]{:S(2)}, u32[]{:S(2)}) collective-permute-start(f32[5,32,16,4]{1,2,3,0:T(8,128)S(1)} %get-tuple-element.59), channel_id=1, source_target_pairs={{0,1},{1,0},{2,3},{3,2},{4,5},{5,4},{6,7},{7,6},{8,9},{9,8},{10,11... | collective-permute-start | bytes 122888 | tf_op jit(solution)/shard_map/ppermute | solution.py:18
  54.3 8.2 %collective-permute-start.7 = (f32[5,32,16,4]{1,2,3,0:T(8,128)S(1)}, f32[5,32,16,4]{1,2,3,0:T(8,128)S(1)}, u32[]{:S(2)}, u32[]{:S(2)}) collective-permute-start(f32[5,32,16,4]{1,2,3,0:T(8,128)S(1)} %get-tuple-element.60), channel_id=1, source_target_pairs={{1,0},{0,1},{3,2},{2,3},{5,4},{4,5},{7,6},{6,7},{9,8},{8,9},{11,10... | collective-permute-start | bytes 122888 | tf_op jit(solution)/shard_map/ppermute | solution.py:20
  72.9 6.1 %copy-start.40 = (f32[40,16,128]{2,1,0:T(8,128)}, f32[40,16,128]{2,1,0:T(8,128)S(1)}, u32[]{:S(2)}) copy-start(f32[40,16,128]{2,1,0:T(8,128)S(1)} %slice_bitcast_fusion.11) | copy-start | bytes 983044
  74.2 4.8 %copy-start.28 = (f32[40,16,128]{2,1,0:T(8,128)}, f32[40,16,128]{2,1,0:T(8,128)S(1)}, u32[]{:S(2)}) copy-start(f32[40,16,128]{2,1,0:T(8,128)S(1)} %slice_bitcast_fusion.10) | copy-start | bytes 983044
  79.0 4.7 %copy-start.18 = (f32[40,16,128]{2,1,0:T(8,128)}, f32[40,16,128]{2,1,0:T(8,128)S(1)}, u32[]{:S(2)}) copy-start(f32[40,16,128]{2,1,0:T(8,128)S(1)} %get-tuple-element.73) | copy-start | bytes 983044
  79.0 4.7 %copy-start.20 = (f32[40,16,128]{2,1,0:T(8,128)}, f32[40,16,128]{2,1,0:T(8,128)S(1)}, u32[]{:S(2)}) copy-start(f32[40,16,128]{2,1,0:T(8,128)S(1)} %get-tuple-element.83) | copy-start | bytes 983044
  79.0 4.7 %copy-start.38 = (f32[40,16,128]{2,1,0:T(8,128)}, f32[40,16,128]{2,1,0:T(8,128)S(1)}, u32[]{:S(2)}) copy-start(f32[40,16,128]{2,1,0:T(8,128)S(1)} %get-tuple-element.72) | copy-start | bytes 983044
  83.7 22.8 %copy-start.48 = (f32[32,8,128]{2,1,0:T(8,128)}, f32[32,8,128]{2,1,0:T(8,128)S(1)}, u32[]{:S(2)}) copy-start(f32[32,8,128]{2,1,0:T(8,128)S(1)} %broadcast.497) | copy-start | bytes 393220
  106.5 6.4 %collective-permute-start.8 = (f32[32,4,128]{2,1,0:T(4,128)S(1)}, f32[32,4,128]{2,1,0:T(4,128)S(1)}, u32[]{:S(2)}, u32[]{:S(2)}) collective-permute-start(f32[32,4,128]{2,1,0:T(4,128)S(1)} %get-tuple-element.93), channel_id=1, source_target_pairs={{0,2},{2,4},{4,6},{6,0},{1,3},{3,5},{5,7},{7,1},{8,10},{10,12},{12... | collective-permute-start | bytes 196616 | tf_op jit(solution)/shard_map/ppermute | solution.py:18
  107.2 5.7 %collective-permute-start.9 = (f32[32,4,128]{2,1,0:T(4,128)S(1)}, f32[32,4,128]{2,1,0:T(4,128)S(1)}, u32[]{:S(2)}, u32[]{:S(2)}) collective-permute-start(f32[32,4,128]{2,1,0:T(4,128)S(1)} %get-tuple-element.94), channel_id=1, source_target_pairs={{2,0},{4,2},{6,4},{0,6},{3,1},{5,3},{7,5},{1,7},{10,8},{12,10},{14... | collective-permute-start | bytes 196616 | tf_op jit(solution)/shard_map/ppermute | solution.py:20
  113.1 1.6 collective-permute-start.10
  113.2 1.9 collective-permute-start.11
  123.4 12.7 %collective-permute-start.12 = (f32[5,32,4,128]{3,1,2,0:T(8,128)}, f32[5,32,4,128]{3,1,2,0:T(8,128)}, u32[]{:S(2)}, u32[]{:S(2)}) collective-permute-start(f32[5,32,4,128]{3,1,2,0:T(8,128)} %copy.56), channel_id=1, source_target_pairs={{0,2},{2,4},{4,6},{6,0},{1,3},{3,5},{5,7},{7,1},{8,10},{10,12},{12... | collective-permute-start | bytes 983048 | tf_op jit(solution)/shard_map/ppermute | solution.py:18
  126.0 16.4 %collective-permute-start.13 = (f32[5,32,4,128]{3,1,2,0:T(8,128)}, f32[5,32,4,128]{3,1,2,0:T(8,128)}, u32[]{:S(2)}, u32[]{:S(2)}) collective-permute-start(f32[5,32,4,128]{3,1,2,0:T(8,128)} %copy.57), channel_id=1, source_target_pairs={{2,0},{4,2},{6,4},{0,6},{3,1},{5,3},{7,5},{1,7},{10,8},{12,10},{14... | collective-permute-start | bytes 983048 | tf_op jit(solution)/shard_map/ppermute | solution.py:20
  144.9 5.9 %copy-start.51 = (f32[8]{0:T(128)S(1)}, f32[8]{0:T(128)}, u32[]{:S(2)}) copy-start(f32[8]{0:T(128)} %param.9) | copy-start | bytes 100
  150.2 23.9 %collective-permute-start.14 = (f32[5,32,16,4]{1,2,3,0:T(8,128)S(1)}, f32[5,32,16,4]{1,2,3,0:T(8,128)S(1)}, u32[]{:S(2)}, u32[]{:S(2)}) collective-permute-start(f32[5,32,16,4]{1,2,3,0:T(8,128)S(1)} %get-tuple-element.57), channel_id=1, source_target_pairs={{0,1},{1,0},{2,3},{3,2},{4,5},{5,4},{6,7},{7,6},{8,9},{9,8},{10,11... | collective-permute-start | bytes 122888 | tf_op jit(solution)/shard_map/ppermute | solution.py:18
  150.3 25.4 %collective-permute-start.15 = (f32[5,32,16,4]{1,2,3,0:T(8,128)S(1)}, f32[5,32,16,4]{1,2,3,0:T(8,128)S(1)}, u32[]{:S(2)}, u32[]{:S(2)}) collective-permute-start(f32[5,32,16,4]{1,2,3,0:T(8,128)S(1)} %get-tuple-element.58), channel_id=1, source_target_pairs={{1,0},{0,1},{3,2},{2,3},{5,4},{4,5},{7,6},{6,7},{9,8},{8,9},{11,10... | collective-permute-start | bytes 122888 | tf_op jit(solution)/shard_map/ppermute | solution.py:20
  186.2 6.4 %copy-start.41 = (f32[40,16,128]{2,1,0:T(8,128)}, f32[40,16,128]{2,1,0:T(8,128)S(1)}, u32[]{:S(2)}) copy-start(f32[40,16,128]{2,1,0:T(8,128)S(1)} %slice_bitcast_fusion.6) | copy-start | bytes 983044
  187.6 5.0 %copy-start.13 = (f32[40,16,128]{2,1,0:T(8,128)}, f32[40,16,128]{2,1,0:T(8,128)S(1)}, u32[]{:S(2)}) copy-start(f32[40,16,128]{2,1,0:T(8,128)S(1)} %slice_bitcast_fusion.4) | copy-start | bytes 983044
  188.0 4.6 %copy-start.29 = (f32[40,16,128]{2,1,0:T(8,128)}, f32[40,16,128]{2,1,0:T(8,128)S(1)}, u32[]{:S(2)}) copy-start(f32[40,16,128]{2,1,0:T(8,128)S(1)} %slice_bitcast_fusion.5) | copy-start | bytes 983044
  192.6 4.4 %copy-start.19 = (f32[40,16,128]{2,1,0:T(8,128)}, f32[40,16,128]{2,1,0:T(8,128)S(1)}, u32[]{:S(2)}) copy-start(f32[40,16,128]{2,1,0:T(8,128)S(1)} %get-tuple-element.68) | copy-start | bytes 983044
  192.6 4.4 %copy-start.21 = (f32[40,16,128]{2,1,0:T(8,128)}, f32[40,16,128]{2,1,0:T(8,128)S(1)}, u32[]{:S(2)}) copy-start(f32[40,16,128]{2,1,0:T(8,128)S(1)} %get-tuple-element.77) | copy-start | bytes 983044
  192.6 4.4 %copy-start.39 = (f32[40,16,128]{2,1,0:T(8,128)}, f32[40,16,128]{2,1,0:T(8,128)S(1)}, u32[]{:S(2)}) copy-start(f32[40,16,128]{2,1,0:T(8,128)S(1)} %get-tuple-element.67) | copy-start | bytes 983044
  (37 other events, 66.5 us)
Sparse Core Ops, SparseCore 0:
  214.0 19.7 all-reduce.5
where the time goes:
time: 248 us; the launch traced here: 243 us
  other arithmetic  84.5 us (34%)
  local copies, waits for them, and re-layouts  58.1 us (23%)
  waiting for transfers between devices  48.2 us (19%)
  starting transfers between devices  19.3 us (8%)
  between operations  16.8 us (7%)
  blocking collectives  15.9 us (6%)
    psum x1, waiting for transfers between devices, body(): return lax.psum(partial_grad, 'rung')  20 us
    ppermute x8, waiting for transfers between devices, with_halo(): lax.ppermute(tail, axis, [(i, (i + 1) % count) for i in range(count)])  19.4 us
    sub x15, other arithmetic, shell_of(): return source_list[outer_reach] - source_list[inner_reach]  19.2 us
    mul x1, other arithmetic, body(): partial_grad = coefficient * (rho_start * pulled_back - weight)  16.2 us
    mul x1, other arithmetic, body(): weight = pore_mask * jnp.exp(correlation - potential)  16.2 us
    unnamed x109, local copies, waits for them, and re-layouts  16 us
    psum x1, blocking collectives, body(): amount = lax.psum(jnp.sum(weight), ('ty', 'tx')) / cell_total  15.9 us
    concatenate x8, other arithmetic, with_halo(): jnp.concatenate([lax.ppermute(tail, axis, [(i, (i + 1) % count) for i in...  13.2 us
  transfers between devices with their start and end apart: 17, of which 12 were waited for; matrix products, arithmetic and copies ran while one was open for 10% of the time, Pallas kernels for 0%

commit v1 on v0

v1 whole, which is shorter than its diff:
```python
import functools
import math

import numpy as np
import ml_dtypes

import jax
import jax.numpy as jnp
from jax import lax
from jax.experimental import pallas as pl
from jax.experimental.pallas import tpu as pltpu
from jax.sharding import PartitionSpec as P

RADIUS = 4
ROWS = 8
TALL = 24
MID = 16
LANES = 128
WIDE = 256
KINDS = 2 * RADIUS + 1
DEPTH = 224
COEF_A = 1.0 / (4.0 * math.pi * RADIUS * RADIUS)
COEF_B = 1.0 / (4.0 * math.pi * RADIUS)
COEF_C = 1.0 / (24.0 * math.pi)


def reach_of(allowed, factor, radius):
    height = -1
    for candidate in range(radius + 1):
        if factor * candidate * candidate <= allowed:
            height = candidate
    return height


def span_count(height):
    return 2 * height + 1 if height >= 0 else 0


def reaches(plane_off, row_off):
    square = plane_off * plane_off + row_off * row_off
    ball = reach_of(RADIUS * RADIUS - square, 1, RADIUS)
    inner = reach_of((2 * RADIUS - 1) ** 2 - 4 * square, 4, RADIUS)
    outer = reach_of((2 * RADIUS + 1) ** 2 - 4 * square, 4, RADIUS)
    return ball, inner, outer


OFFS = range(-RADIUS, RADIUS + 1)
SHELL = sum(
    span_count(reaches(p, s)[2]) - span_count(reaches(p, s)[1]) for p in OFFS for s in OFFS
)
AREA = 4.0 * math.pi * RADIUS * RADIUS / SHELL
VEC = AREA / RADIUS


def shell_terms(p, s):
    _, inner, outer = reaches(p, s)
    terms = []
    if outer >= 0:
        terms.append((outer, 1))
    if inner >= 0:
        terms.append((inner, -1))
    return terms


def column_matrix():
    mat = np.zeros((KINDS, WIDE, WIDE), np.float32)
    for out in range(WIDE):
        for h in OFFS:
            src = (out + h) % WIDE
            for k in range(abs(h), RADIUS + 1):
                mat[k, src, out] = 1
                if k > 0:
                    mat[RADIUS + k, src, out] = h
    return mat


def spread_rows():
    mat = np.zeros((4, RADIUS + 1, MID, DEPTH), np.float32)
    for p in range(RADIUS + 1):
        for s in OFFS:
            ball = reaches(p, s)[0]
            for r in range(MID):
                src = r + RADIUS + s
                if ball >= 0:
                    mat[0, p, r, ball * TALL + src] += 1
                for k, sign in shell_terms(p, s):
                    mat[1, p, r, k * TALL + src] += sign
                    mat[2, p, r, k * TALL + src] += s * sign
                    if k > 0:
                        mat[3, p, r, (RADIUS + k) * TALL + src] += sign
    flat = mat.reshape(4 * (RADIUS + 1) * MID, DEPTH)
    return np.concatenate([flat, flat], axis=1)


def collect_rows():
    full = np.zeros((KINDS, KINDS, ROWS, 5 * MID), np.float32)
    for p in OFFS:
        for s in OFFS:
            ball = reaches(p, s)[0]
            for r in range(ROWS):
                src = r + RADIUS + s
                if ball >= 0:
                    full[ball, p + RADIUS, r, src] += 1
                for k, sign in shell_terms(p, s):
                    full[k, p + RADIUS, r, MID + src] += sign
                    full[k, p + RADIUS, r, 2 * MID + src] += p * sign
                    full[k, p + RADIUS, r, 3 * MID + src] += s * sign
                    if k > 0:
                        full[RADIUS + k, p + RADIUS, r, 4 * MID + src] += sign
    used = [(k, p) for k in range(KINDS) for p in range(KINDS) if np.any(full[k, p])]
    flat = np.concatenate([full[k, p] for k, p in used], axis=0)
    return used, np.concatenate([flat, flat], axis=1)


COLS = column_matrix()
USED, BACK = collect_rows()
GROUPS = 4 * (RADIUS + 1)
BF = ml_dtypes.bfloat16
COLS_FWD = np.concatenate([COLS[k] for k in range(1, KINDS)], axis=1).astype(BF)
COLS_BACK = np.concatenate([COLS[k][:, :LANES] for k in range(KINDS)], axis=0).astype(BF)
FRONT = spread_rows().astype(BF)
BACK = BACK.astype(BF)
N_BACK = len(USED) * ROWS


def split(x):
    high = x.astype(jnp.bfloat16)
    low = (x - high.astype(jnp.float32)).astype(jnp.bfloat16)
    return high, low


def dot(a, b):
    return jnp.dot(a, b, preferred_element_type=jnp.float32)


def columns_forward(planes, x_ref, cols_ref, c_ref):
    x = x_ref[...].reshape(planes * TALL, WIDE)
    c_ref[:, 0:WIDE] = x
    high, low = split(x)
    for k in range(1, KINDS):
        mat = cols_ref[:, (k - 1) * WIDE : k * WIDE]
        c_ref[:, k * WIDE : (k + 1) * WIDE] = dot(high, mat) + dot(low, mat)


def rows_forward(planes, c_ref, front_ref, y_ref):
    zeros = jnp.zeros((RADIUS, GROUPS * MID, WIDE), jnp.float32)
    y_ref[0:RADIUS] = zeros
    y_ref[RADIUS + planes :] = zeros

    def step(q, carry):
        start = pl.multiple_of(q * TALL, TALL)
        parts = [c_ref[pl.ds(start, TALL), k * WIDE : (k + 1) * WIDE] for k in range(KINDS)]
        parts.append(jnp.zeros((DEPTH - KINDS * TALL, WIDE), jnp.float32))
        high, low = split(jnp.concatenate(parts, axis=0))
        y_ref[q + RADIUS] = dot(front_ref[...], jnp.concatenate([high, low], axis=0))
        return carry

    lax.fori_loop(0, planes, step, 0, unroll=4)


def densities_at(q, y_ref):
    def get(group, p, off):
        row = (group * (RADIUS + 1) + p) * MID
        return y_ref[q + RADIUS + off, row : row + MID, :]

    volume, surface, rows, cols = [get(g, 0, 0) for g in range(4)]
    plane = jnp.zeros_like(volume)
    for p in range(1, RADIUS + 1):
        volume = volume + (get(0, p, p) + get(0, p, -p))
        after, before = get(1, p, p), get(1, p, -p)
        surface = surface + (after + before)
        plane = plane + p * (after - before)
        rows = rows + (get(2, p, p) + get(2, p, -p))
        cols = cols + (get(3, p, p) + get(3, p, -p))
    return volume, AREA * surface, VEC * plane, VEC * rows, VEC * cols


def derivs_of(n3, n2, vp, vr, vc):
    free = 1.0 - n3
    inv = 1.0 / free
    sq = vp * vp + vr * vr + vc * vc
    u = n2 * n2 - sq
    w = n2 * (u - 2.0 * sq)
    d3 = inv * (COEF_A * n2 + inv * (COEF_B * u + inv * (2.0 * COEF_C) * w))
    d2 = -COEF_A * jnp.log(free) + inv * (2.0 * COEF_B * n2 + inv * (3.0 * COEF_C) * u)
    dv = -inv * (2.0 * COEF_B + inv * (6.0 * COEF_C) * n2)
    return d3, d2, dv * vp, dv * vr, dv * vc


def hess_of(dens, images):
    n3, n2, vp, vr, vc = dens
    m3, m2, mp, mr, mc = images
    inv = 1.0 / (1.0 - n3)
    sq = vp * vp + vr * vr + vc * vc
    u = n2 * n2 - sq
    w = n2 * (u - 2.0 * sq)
    vm = vp * mp + vr * mr + vc * mc
    h33 = inv * inv * (COEF_A * n2 + inv * (2.0 * COEF_B * u + inv * (6.0 * COEF_C) * w))
    h32 = inv * (COEF_A + inv * (2.0 * COEF_B * n2 + inv * (6.0 * COEF_C) * u))
    h3v = inv * inv * (2.0 * COEF_B + inv * (12.0 * COEF_C) * n2)
    h2v = 6.0 * COEF_C * inv * inv
    h22 = inv * (2.0 * COEF_B + inv * (6.0 * COEF_C) * n2)
    mix = h3v * m3 + h2v * m2
    return (
        h33 * m3 + h32 * m2 - h3v * vm,
        h32 * m3 + h22 * m2 - h2v * vm,
        -mix * vp - h22 * mp,
        -mix * vr - h22 * mr,
        -mix * vc - h22 * mc,
    )


def push_back(q, fields, back_ref, z_ref):
    g3, g2, gp, gr, gc = fields
    stacked = jnp.concatenate([g3, AREA * g2, -VEC * gp, -VEC * gr, -VEC * gc], axis=0)
    high, low = split(stacked)
    z_ref[q + RADIUS] = dot(back_ref[...], jnp.concatenate([high, low], axis=0))


def columns_back(planes, z_ref, cols_ref, d_ref):
    def step(q, carry):
        start = pl.multiple_of(q * ROWS, ROWS)
        for k in range(KINDS):
            total = None
            for place, (kind, off) in enumerate(USED):
                if kind == k:
                    term = z_ref[q + off, place * ROWS : (place + 1) * ROWS, :]
                    total = term if total is None else total + term
            d_ref[pl.ds(start, ROWS), k * WIDE : (k + 1) * WIDE] = total
        return carry

    lax.fori_loop(0, planes, step, 0, unroll=2)
    out = None
    for k in range(KINDS):
        high, low = split(d_ref[:, k * WIDE : (k + 1) * WIDE])
        mat = cols_ref[k * WIDE : (k + 1) * WIDE, :]
        term = dot(high, mat) + dot(low, mat)
        out = term if out is None else out + term
    return out.reshape(planes, ROWS, LANES)


def clear_edges(planes, z_ref):
    zeros = jnp.zeros((RADIUS, N_BACK, WIDE), jnp.float32)
    z_ref[0:RADIUS] = zeros
    z_ref[RADIUS + planes :] = zeros


def first_kernel(
    planes, x_ref, pot_ref, lab_ref, cols_ref, front_ref, back_ref, colsb_ref,
    weight_ref, dens_ref, c_ref, y_ref, z_ref, d_ref,
):
    columns_forward(planes, x_ref, cols_ref, c_ref)
    rows_forward(planes, c_ref, front_ref, y_ref)
    clear_edges(planes, z_ref)

    def step(q, carry):
        dens = densities_at(q, y_ref)
        for i in range(5):
            dens_ref[q, i * MID : (i + 1) * MID, :] = dens[i]
        push_back(q, derivs_of(*dens), back_ref, z_ref)
        return carry

    lax.fori_loop(0, planes, step, 0, unroll=2)
    total = columns_back(planes, z_ref, colsb_ref, d_ref)
    mask = lab_ref[...].astype(jnp.float32)
    weight_ref[...] = mask * jnp.exp(-total - pot_ref[...])


def second_kernel(
    planes, x_ref, dens_ref, rho_ref, coef_ref, cols_ref, front_ref, back_ref, colsb_ref,
    out_ref, c_ref, y_ref, z_ref, d_ref,
):
    columns_forward(planes, x_ref, cols_ref, c_ref)
    rows_forward(planes, c_ref, front_ref, y_ref)
    clear_edges(planes, z_ref)

    def step(q, carry):
        images = densities_at(q, y_ref)
        dens = [dens_ref[q, i * MID : (i + 1) * MID, :] for i in range(5)]
        push_back(q, hess_of(dens, images), back_ref, z_ref)
        return carry

    lax.fori_loop(0, planes, step, 0, unroll=2)
    total = columns_back(planes, z_ref, colsb_ref, d_ref)
    weight = x_ref[:, ROWS : 2 * ROWS, 0:LANES]
    out_ref[...] = coef_ref[0] * (rho_ref[...] * total - weight)


def scratch(planes):
    return [
        pltpu.VMEM((planes * TALL, KINDS * WIDE), jnp.float32),
        pltpu.VMEM((planes + 2 * RADIUS, GROUPS * MID, WIDE), jnp.float32),
        pltpu.VMEM((planes + 2 * RADIUS, N_BACK, WIDE), jnp.float32),
        pltpu.VMEM((planes * ROWS, KINDS * WIDE), jnp.float32),
    ]


PARAMS = pltpu.CompilerParams(vmem_limit_bytes=58 * 1024 * 1024)
VM = pl.BlockSpec(memory_space=pltpu.VMEM)
SM = pl.BlockSpec(memory_space=pltpu.SMEM)


def gather_tiles(tile):
    count = lax.axis_size("ty")
    ahead = [(i, (i + 1) % count) for i in range(count)]
    above = lax.ppermute(tile, "ty", ahead)
    below = lax.ppermute(tile, "ty", [(j, i) for i, j in ahead])
    tall = jnp.concatenate([above, tile, below], axis=1)
    other = lax.ppermute(tall, "tx", [(0, 1), (1, 0)])
    return jnp.concatenate([tall, other], axis=2)


def lookup(table_vals, chosen):
    return jnp.sum(jnp.where(jnp.arange(table_vals.shape[0]) == chosen, table_vals, 0.0))


def body(potential, labels, rung_mu, mu_table, target_table):
    planes = potential.shape[0]
    pore_mask = labels.astype(jnp.float32)
    chem_pot = lookup(mu_table, rung_mu[0])
    target = lookup(target_table, rung_mu[0])
    rho = pore_mask * jnp.exp(chem_pot - potential)
    mats = [jnp.asarray(m) for m in (COLS_FWD, FRONT, BACK, COLS_BACK)]
    weight, dens = pl.pallas_call(
        functools.partial(first_kernel, planes),
        out_shape=(
            jax.ShapeDtypeStruct(potential.shape, jnp.float32),
            jax.ShapeDtypeStruct((planes, 5 * MID, WIDE), jnp.float32),
        ),
        in_specs=[VM] * 7,
        out_specs=(VM, VM),
        scratch_shapes=scratch(planes),
        compiler_params=PARAMS,
    )(gather_tiles(rho), potential, labels, *mats)
    cell_total = weight.size * lax.axis_size("ty") * lax.axis_size("tx")
    amount = lax.psum(jnp.sum(weight), ("ty", "tx")) / cell_total
    coefficient = jnp.log(amount / target) / amount
    grad = pl.pallas_call(
        functools.partial(second_kernel, planes),
        out_shape=jax.ShapeDtypeStruct(potential.shape, jnp.float32),
        in_specs=[VM] * 3 + [SM] + [VM] * 4,
        out_specs=VM,
        scratch_shapes=scratch(planes),
        compiler_params=PARAMS,
    )(gather_tiles(weight), dens, rho, coefficient[None], *mats)
    return lax.psum(grad, "rung")


def solution(mesh):
    return jax.shard_map(
        body,
        mesh=mesh,
        in_specs=(P("parts", "ty", "tx"), P("parts", "ty", "tx"), P(("parts", "rung")), P(), P()),
        out_specs=P("parts", "ty", "tx"),
        check_vma=False,
    )
```

time: 248 us -> 118 us (0.48); the launches traced: 243 us -> 118 us
  other arithmetic: 84.5 us -> 7.05 us
  local copies, waits for them, and re-layouts: 58.1 us -> 1.6 us
  Pallas kernels: 0 us -> 35.4 us
  waiting for transfers between devices: 48.2 us -> 32.9 us
  starting transfers between devices: 19.3 us -> 9.07 us
    pallas_call x0 -> x2, Pallas kernels: none -> 35.4 us  [the longest x1 18.2 us: body(): pl.pallas_call(functools.partial(second_kernel, planes), out_shape=jax.Sh...]
    mul x5 -> x1, other arithmetic: 35.5 us -> 1.64 us  [body(): rho = pore_mask * jnp.exp(chem_pot - potential)]
    sub x15 -> x0, other arithmetic: 19.2 us -> none  [shell_of(): return source_list[outer_reach] - source_list[inner_reach]]
    ppermute x8 -> x0, local copies, waits for them, and re-layouts: 16.3 us -> none  [the longest x4 8.16 us: with_halo(): lax.ppermute(tail, axis, [(i, (i + 1) % count) for i in range(count)])]
    ppermute x16 -> x6, waiting for transfers between devices: 28.2 us -> 13.1 us  [the longest x2 7.45 us: gather_tiles(): above = lax.ppermute(tile, 'ty', ahead)]
    unnamed x109 -> x6, local copies, waits for them, and re-layouts: 16 us -> 1.59 us
    concatenate x8 -> x3, other arithmetic: 13.2 us -> 1.93 us  [the longest x2 1.89 us: gather_tiles(): return jnp.concatenate([tall, other], axis=2)]
    concatenate x2 -> x1, local copies, waits for them, and re-layouts: 10.8 us -> 0.01 us  [gather_tiles(): tall = jnp.concatenate([above, tile, below], axis=1)]
  transfers between devices with their start and end apart: 17 -> 7, of which waited for: 12 -> 5; matrix products, arithmetic and copies ran while one was open for 10% -> 2% of each run, Pallas kernels for 0% -> 0%
where the time goes in v1:
time: 118 us
  Pallas kernels  35.4 us (30%)
  waiting for transfers between devices  32.9 us (28%)
  blocking collectives  15.9 us (13%)
  between operations  15.5 us (13%)
  starting transfers between devices  9.07 us (8%)
  other arithmetic  7.05 us (6%)
  local copies, waits for them, and re-layouts  1.6 us (1%)
    psum x1, waiting for transfers between devices, body(): return lax.psum(grad, 'rung')  19.9 us
    pallas_call x1, Pallas kernels, body(): pl.pallas_call(functools.partial(second_kernel, planes), out_shape=jax.Sh...  18.2 us
    pallas_call x1, Pallas kernels, body(): pl.pallas_call(functools.partial(first_kernel, planes), out_shape=(jax.Sh...  17.2 us
    psum x1, blocking collectives, body(): amount = lax.psum(jnp.sum(weight), ('ty', 'tx')) / cell_total  15.9 us
    ppermute x2, starting transfers between devices, gather_tiles(): below = lax.ppermute(tile, 'ty', [(j, i) for i, j in ahead])  7.6 us
    ppermute x2, waiting for transfers between devices, gather_tiles(): above = lax.ppermute(tile, 'ty', ahead)  7.45 us
    ppermute x2, waiting for transfers between devices, gather_tiles(): below = lax.ppermute(tile, 'ty', [(j, i) for i, j in ahead])  3.9 us
  transfers between devices with their start and end apart: 7, of which 5 were waited for; matrix products, arithmetic and copies ran while one was open for 2% of the time, Pallas kernels for 0%

profile of v1, /device:TPU:0, one launch (start us, length us, event | category | flops | bytes accessed | tf_op | source)
XLA Modules:
  0.0 117.5 jit_solution(12172310634825732474)
XLA Ops:
  6.5 0.0 all-reduce.2.cloned.1.call-start
  7.2 1.3 %fusion = f32[]{:T(128)} fusion(f32[8]{0:T(128)} %param.12, s32[]{:T(128)} %bitcast.2), kind=kLoop, calls=%fused_computation.9 | loop fusion | flops 23 | bytes 40 | tf_op jit(solution)/shard_map/reduce_sum | solution.py:314
  8.5 1.6 %exponential_multiply_fusion.rho_ref = f32[32,8,128]{2,1,0:T(8,128)S(1)} fusion(f32[32,8,128]{2,1,0:T(8,128)} %pot_ref.1, s32[32,8,128]{2,1,0:T(8,128)} %lab_ref.1, f32[]{:T(128)} %fusion), kind=kLoop, calls=%fused_computation.3 | loop fusion | flops 98304 | bytes 393220 | tf_op jit(solution)/shard_map/mul | solution.py:322
  10.1 0.0 copy-start
  10.1 5.1 %collective-permute-start.1 = (f32[32,8,128]{2,1,0:T(8,128)S(1)}, f32[32,8,128]{2,1,0:T(8,128)S(1)}, u32[]{:S(2)}, u32[]{:S(2)}) collective-permute-start(f32[32,8,128]{2,1,0:T(8,128)S(1)} %exponential_multiply_fusion.rho_ref), channel_id=1, source_target_pairs={{2,0},{4,2},{6,4},{0,6},{3,1},{5,3},{7,5},{1,7},{10,8},{12,10},{14... | collective-permute-start | bytes 393224 | tf_op jit(solution)/shard_map/ppermute | solution.py:307
  15.2 0.0 collective-permute-start
  15.2 3.9 %collective-permute-done.1 = f32[32,8,128]{2,1,0:T(8,128)S(1)} collective-permute-done((f32[32,8,128]{2,1,0:T(8,128)S(1)}, f32[32,8,128]{2,1,0:T(8,128)S(1)}, u32[]{:S(2)}, u32[]{:S(2)}) %collective-permute-start.1) | collective-permute-done | bytes 131104 | tf_op jit(solution)/shard_map/ppermute | solution.py:307
  19.1 2.9 %collective-permute-done = f32[32,8,128]{2,1,0:T(8,128)S(1)} collective-permute-done((f32[32,8,128]{2,1,0:T(8,128)S(1)}, f32[32,8,128]{2,1,0:T(8,128)S(1)}, u32[]{:S(2)}, u32[]{:S(2)}) %collective-permute-start) | collective-permute-done | bytes 131104 | tf_op jit(solution)/shard_map/ppermute | solution.py:306
  22.0 0.0 copy-start.1
  22.0 0.1 collective-permute-start.2
  22.1 1.7 %collective-permute-done.2 = f32[32,24,128]{2,1,0:T(8,128)S(1)} collective-permute-done((f32[32,24,128]{2,1,0:T(8,128)S(1)}, f32[32,24,128]{2,1,0:T(8,128)S(1)}, u32[]{:S(2)}, u32[]{:S(2)}) %collective-permute-start.2) | collective-permute-done | bytes 393248 | tf_op jit(solution)/shard_map/ppermute | solution.py:309
  23.8 0.9 pad_maximum_fusion.x_ref
  24.8 17.2 %shard_map.91 = (f32[32,8,128]{2,1,0:T(8,128)}, f32[32,80,256]{2,1,0:T(8,128)}) custom-call(f32[32,24,256]{2,1,0:T(8,128)} %pad_maximum_fusion.x_ref, f32[32,8,128]{2,1,0:T(8,128)} %pot_ref.1, s32[32,8,128]{2,1,0:T(8,128)} %lab_ref.1, bf16[256,2048]{1,0:T(8,128)(2,1)} %constant.13.clone.cols_ref, bf16[320,448]{1,0:T(8,128)(2,1)} %constant.14.clone.front_ref, ...), custom_call_target="tpu_custom_call" | custom-call | tf_op jit(solution)/shard_map/pallas_call | solution.py:324
  42.0 0.0 copy-done
  42.0 1.3 %collective-permute-start.3 = (f32[32,8,128]{2,1,0:T(8,128)}, f32[32,8,128]{2,1,0:T(8,128)S(1)}, u32[]{:S(2)}, u32[]{:S(2)}) collective-permute-start(f32[32,8,128]{2,1,0:T(8,128)} %get-tuple-element.7), channel_id=1, source_target_pairs={{0,2},{2,4},{4,6},{6,0},{1,3},{3,5},{5,7},{7,1},{8,10},{10,12},{12... | collective-permute-start | bytes 393224 | tf_op jit(solution)/shard_map/ppermute | solution.py:306
  43.3 2.5 %collective-permute-start.4 = (f32[32,8,128]{2,1,0:T(8,128)}, f32[32,8,128]{2,1,0:T(8,128)S(1)}, u32[]{:S(2)}, u32[]{:S(2)}) collective-permute-start(f32[32,8,128]{2,1,0:T(8,128)} %get-tuple-element.7), channel_id=1, source_target_pairs={{2,0},{4,2},{6,4},{0,6},{3,1},{5,3},{7,5},{1,7},{10,8},{12,10},{14... | collective-permute-start | bytes 393224 | tf_op jit(solution)/shard_map/ppermute | solution.py:307
  45.8 4.6 %collective-permute-done.3 = f32[32,8,128]{2,1,0:T(8,128)S(1)} collective-permute-done((f32[32,8,128]{2,1,0:T(8,128)}, f32[32,8,128]{2,1,0:T(8,128)S(1)}, u32[]{:S(2)}, u32[]{:S(2)}) %collective-permute-start.3) | collective-permute-done | bytes 131104 | tf_op jit(solution)/shard_map/ppermute | solution.py:306
  50.4 1.6 %fusion.2 = (f32[]{:T(128)}, f32[32,24,128]{2,1,0:T(8,128)S(1)}) fusion(f32[32,8,128]{2,1,0:T(8,128)} %get-tuple-element.7, f32[32,24,128]{2,1,0:T(8,128)S(1)} %constant_dynamic-update-slice_fusion.2), kind=kLoop, calls=%fused_computation.11 | loop fusion | flops 32767 | bytes 262148 | tf_op jit(solution)/shard_map/reduce_sum | solution.py:336
  52.0 0.0 collective-permute-done.4
  52.0 0.1 collective-permute-start.5
  52.1 0.0 copy-done.1
  52.1 0.7 fusion.1
  52.7 15.9 %psum.14 = f32[]{:T(128)} all-reduce(f32[]{:T(128)} %get-tuple-element.9), channel_id=1, replica_groups=mesh['parts'=2,'rung'=2,'ty'=4,'tx'=2] {'ty','tx'}, use_global_device_ids=true, to_apply=%region_2.3 | all-reduce | flops 1 | bytes 8 | tf_op jit(solution)/shard_map/psum | solution.py:336
  70.1 0.0 collective-permute-done.5
  70.1 0.9 pad_maximum_fusion.1.x_ref
  71.0 18.2 %shard_map.92 = f32[32,8,128]{2,1,0:T(8,128)} custom-call(f32[32,24,256]{2,1,0:T(8,128)} %pad_maximum_fusion.1.x_ref, f32[32,80,256]{2,1,0:T(8,128)} %get-tuple-element.8.dens_ref, f32[32,8,128]{2,1,0:T(8,128)} %copy-done, f32[1]{0:T(128)} %bitcast.1.coef_ref, bf16[256,2048]{1,0:T(8,128)(2,1)} %constant.13.clone.cols_ref, ...), custom_call_target="tpu_custom_call" | custom-call | tf_op jit(solution)/shard_map/pallas_call | solution.py:338
  89.2 0.0 all-reduce.2.cloned.1.call-update
  89.3 19.9 %all-reduce.2.cloned.1.call-done = f32[32,8,128]{2,1,0:T(8,128)} async-done(((f32[32,8,128]{2,1,0:T(8,128)}), f32[32,8,128]{2,1,0:T(8,128)}) %all-reduce.2.cloned.1.call-update) | async-done | bytes 131088 | tf_op jit(solution)/shard_map/psum | solution.py:346
  109.1 1.6 %copy.14 = f32[32,8,128]{2,1,0:T(8,128)} copy(f32[32,8,128]{2,1,0:T(8,128)} %all-reduce.2.cloned.1.call-done) | data formatting | bytes 262144
  (3 shorter events, 0.1 us)
Async XLA Ops:
  6.5 102.6 %all-reduce.2.cloned.1.call-start = ((), (), s32[]{:S(2)}) async-start(), calls=%async_computation | async-start | bytes 262144 | tf_op jit(solution)/shard_map/psum | solution.py:346
  10.1 31.9 %copy-start = (f32[32,8,128]{2,1,0:T(8,128)}, f32[32,8,128]{2,1,0:T(8,128)S(1)}, u32[]{:S(2)}) copy-start(f32[32,8,128]{2,1,0:T(8,128)S(1)} %exponential_multiply_fusion.rho_ref) | copy-start | bytes 393220
  10.1 9.0 %collective-permute-start.1 = (f32[32,8,128]{2,1,0:T(8,128)S(1)}, f32[32,8,128]{2,1,0:T(8,128)S(1)}, u32[]{:S(2)}, u32[]{:S(2)}) collective-permute-start(f32[32,8,128]{2,1,0:T(8,128)S(1)} %exponential_multiply_fusion.rho_ref), channel_id=1, source_target_pairs={{2,0},{4,2},{6,4},{0,6},{3,1},{5,3},{7,5},{1,7},{10,8},{12,10},{14... | collective-permute-start | bytes 393224 | tf_op jit(solution)/shard_map/ppermute | solution.py:307
  15.2 6.8 %collective-permute-start = (f32[32,8,128]{2,1,0:T(8,128)S(1)}, f32[32,8,128]{2,1,0:T(8,128)S(1)}, u32[]{:S(2)}, u32[]{:S(2)}) collective-permute-start(f32[32,8,128]{2,1,0:T(8,128)S(1)} %exponential_multiply_fusion.rho_ref), channel_id=1, source_target_pairs={{0,2},{2,4},{4,6},{6,0},{1,3},{3,5},{5,7},{7,1},{8,10},{10,12},{12... | collective-permute-start | bytes 393224 | tf_op jit(solution)/shard_map/ppermute | solution.py:306
  22.0 30.0 %copy-start.1 = (f32[8]{0:T(128)S(1)}, f32[8]{0:T(128)}, u32[]{:S(2)}) copy-start(f32[8]{0:T(128)} %param.13) | copy-start | bytes 100
  22.0 1.8 %collective-permute-start.2 = (f32[32,24,128]{2,1,0:T(8,128)S(1)}, f32[32,24,128]{2,1,0:T(8,128)S(1)}, u32[]{:S(2)}, u32[]{:S(2)}) collective-permute-start(f32[32,24,128]{2,1,0:T(8,128)S(1)} %pad_maximum_fusion.2), channel_id=1, source_target_pairs={{0,1},{1,0},{2,3},{3,2},{4,5},{5,4},{6,7},{7,6},{8,9},{9,8},{10,11... | collective-permute-start | bytes 1179656 | tf_op jit(solution)/shard_map/ppermute | solution.py:309
  42.0 8.4 %collective-permute-start.3 = (f32[32,8,128]{2,1,0:T(8,128)}, f32[32,8,128]{2,1,0:T(8,128)S(1)}, u32[]{:S(2)}, u32[]{:S(2)}) collective-permute-start(f32[32,8,128]{2,1,0:T(8,128)} %get-tuple-element.7), channel_id=1, source_target_pairs={{0,2},{2,4},{4,6},{6,0},{1,3},{3,5},{5,7},{7,1},{8,10},{10,12},{12... | collective-permute-start | bytes 393224 | tf_op jit(solution)/shard_map/ppermute | solution.py:306
  43.3 8.7 %collective-permute-start.4 = (f32[32,8,128]{2,1,0:T(8,128)}, f32[32,8,128]{2,1,0:T(8,128)S(1)}, u32[]{:S(2)}, u32[]{:S(2)}) collective-permute-start(f32[32,8,128]{2,1,0:T(8,128)} %get-tuple-element.7), channel_id=1, source_target_pairs={{2,0},{4,2},{6,4},{0,6},{3,1},{5,3},{7,5},{1,7},{10,8},{12,10},{14... | collective-permute-start | bytes 393224 | tf_op jit(solution)/shard_map/ppermute | solution.py:307
  52.0 18.1 %collective-permute-start.5 = (f32[32,24,128]{2,1,0:T(8,128)S(1)}, f32[32,24,128]{2,1,0:T(8,128)S(1)}, u32[]{:S(2)}, u32[]{:S(2)}) collective-permute-start(f32[32,24,128]{2,1,0:T(8,128)S(1)} %constant_dynamic-update-slice_fusion), channel_id=1, source_target_pairs={{0,1},{1,0},{2,3},{3,2},{4,5},{5,4},{6,7},{7,6},{8,9},{9,8},{10,11... | collective-permute-start | bytes 1179656 | tf_op jit(solution)/shard_map/ppermute | solution.py:309
Sparse Core Ops, SparseCore 0:
  89.4 19.6 all-reduce.1

commit v2 on v1

--- a/solution.py
+++ b/solution.py
@@ -267,7 +267,7 @@
 
 
 def second_kernel(
-    planes, x_ref, dens_ref, rho_ref, coef_ref, cols_ref, front_ref, back_ref, colsb_ref,
+    planes, cells, x_ref, dens_ref, rho_ref, sum_ref, rung_ref, table_ref, cols_ref, front_ref, back_ref, colsb_ref,
     out_ref, c_ref, y_ref, z_ref, d_ref,
 ):
     columns_forward(planes, x_ref, cols_ref, c_ref)
@@ -283,7 +283,11 @@
     lax.fori_loop(0, planes, step, 0, unroll=2)
     total = columns_back(planes, z_ref, colsb_ref, d_ref)
     weight = x_ref[:, ROWS : 2 * ROWS, 0:LANES]
-    out_ref[...] = coef_ref[0] * (rho_ref[...] * total - weight)
+    rho = rho_ref[:, ROWS : 2 * ROWS, 0:LANES]
+    amount = jnp.sum(sum_ref[...], axis=(0, 1), keepdims=True) * (1.0 / cells)
+    amount = jnp.broadcast_to(amount, (ROWS, LANES))
+    coefficient = jnp.log(amount / pick(rung_ref[0], table_ref)) / amount
+    out_ref[...] = coefficient[None] * (rho * total - weight)
 
 
 def scratch(planes):
@@ -300,50 +304,182 @@
 SM = pl.BlockSpec(memory_space=pltpu.SMEM)
 
 
-def gather_tiles(tile):
+MESH = pl.DeviceIdType.MESH
+
+
+def pick(index, table_ref):
+    total = jnp.float32(0.0)
+    for i in range(table_ref.shape[0]):
+        total = total + jnp.where(index == i, table_ref[i], jnp.float32(0.0))
+    return total
+
+
+def swap_tiles(x_ref, send_sem, recv_sem):
     count = lax.axis_size("ty")
-    ahead = [(i, (i + 1) % count) for i in range(count)]
-    above = lax.ppermute(tile, "ty", ahead)
-    below = lax.ppermute(tile, "ty", [(j, i) for i, j in ahead])
-    tall = jnp.concatenate([above, tile, below], axis=1)
-    other = lax.ppermute(tall, "tx", [(0, 1), (1, 0)])
-    return jnp.concatenate([tall, other], axis=2)
-
-
-def lookup(table_vals, chosen):
-    return jnp.sum(jnp.where(jnp.arange(table_vals.shape[0]) == chosen, table_vals, 0.0))
+    ty, tx = lax.axis_index("ty"), lax.axis_index("tx")
+    own = x_ref.at[:, ROWS : 2 * ROWS, 0:LANES]
+
+    def copy(i, src, rows, lane, device):
+        dst = x_ref.at[:, rows : rows + ROWS, lane : lane + LANES]
+        return pltpu.make_async_remote_copy(
+            src_ref=src, dst_ref=dst, send_sem=send_sem.at[i], recv_sem=recv_sem.at[i],
+            device_id=device, device_id_type=MESH,
+        )
+
+    beside = {"tx": 1 - tx}
+    down = copy(0, own, 0, 0, {"ty": lax.rem(ty + 1, count)})
+    up = copy(1, own, 2 * ROWS, 0, {"ty": lax.rem(ty + count - 1, count)})
+    side = copy(2, own, ROWS, LANES, beside)
+    down.start()
+    up.start()
+    side.start()
+    head = copy(3, x_ref.at[:, 0:ROWS, 0:LANES], 0, LANES, beside)
+    tail = copy(4, x_ref.at[:, 2 * ROWS : 3 * ROWS, 0:LANES], 2 * ROWS, LANES, beside)
+    down.wait_recv()
+    head.start()
+    up.wait_recv()
+    tail.start()
+    down.wait_send()
+    up.wait_send()
+    side.wait()
+    head.wait()
+    tail.wait()
+
+
+def greet(devices):
+    barrier = pltpu.get_barrier_semaphore()
+    for device in devices:
+        pl.semaphore_signal(barrier, inc=1, device_id=device, device_id_type=MESH)
+    pl.semaphore_wait(barrier, len(devices))
+
+
+def start_kernel(pot_ref, lab_ref, rung_ref, table_ref, x_ref, send_sem, recv_sem):
+    count = lax.axis_size("ty")
+    ty, tx = lax.axis_index("ty"), lax.axis_index("tx")
+    chem_pot = pick(rung_ref[0], table_ref)
+    mask = lab_ref[...].astype(jnp.float32)
+    x_ref[:, ROWS : 2 * ROWS, 0:LANES] = mask * jnp.exp(chem_pot - pot_ref[...])
+    greet([
+        {"ty": lax.rem(ty + 1, count)}, {"ty": lax.rem(ty + count - 1, count)}, {"tx": 1 - tx},
+    ])
+    swap_tiles(x_ref, send_sem, recv_sem)
+
+
+def weight_kernel(
+    weight_ref, x_ref, sum_ref, slots, send_sem, recv_sem, part_send, part_recv,
+):
+    cores = lax.axis_size("tx")
+    group = lax.axis_size("ty") * cores
+    me = lax.axis_index("ty") * cores + lax.axis_index("tx")
+    others = []
+    for j in range(1, group):
+        target = lax.rem(me + j, group)
+        others.append({"ty": target // cores, "tx": lax.rem(target, cores)})
+    weight = weight_ref[...]
+    x_ref[:, ROWS : 2 * ROWS, 0:LANES] = weight
+    slots[0] = jnp.sum(weight, axis=0)
+    greet(others)
+    copies = []
+    for j in range(1, group):
+        copies.append(pltpu.make_async_remote_copy(
+            src_ref=slots.at[0], dst_ref=slots.at[j],
+            send_sem=part_send.at[j], recv_sem=part_recv.at[j],
+            device_id=others[j - 1], device_id_type=MESH,
+        ))
+        copies[-1].start()
+    swap_tiles(x_ref, send_sem, recv_sem)
+    for copy in copies:
+        copy.wait()
+    total = slots[0]
+    for j in range(1, group):
+        total = total + slots[j]
+    sum_ref[...] = total
+
+
+def rung_kernel(grad_ref, out_ref, slots, send_sem, recv_sem):
+    count = lax.axis_size("rung")
+    me = lax.axis_index("rung")
+    others = [{"rung": lax.rem(me + j, count)} for j in range(1, count)]
+    greet(others)
+    copies = []
+    for j in range(1, count):
+        copies.append(pltpu.make_async_remote_copy(
+            src_ref=grad_ref, dst_ref=slots.at[j - 1],
+            send_sem=send_sem.at[j - 1], recv_sem=recv_sem.at[j - 1],
+            device_id=others[j - 1], device_id_type=MESH,
+        ))
+        copies[-1].start()
+    for copy in copies:
+        copy.wait()
+    total = grad_ref[...]
+    for j in range(1, count):
+        total = total + slots[j - 1]
+    out_ref[...] = total
+
+
+def talks(place):
+    return pltpu.CompilerParams(
+        collective_id=place, has_side_effects=True, vmem_limit_bytes=24 * 1024 * 1024
+    )
+
+
+def dma(count):
+    return pltpu.SemaphoreType.DMA((count,))
 
 
 def body(potential, labels, rung_mu, mu_table, target_table):
     planes = potential.shape[0]
-    pore_mask = labels.astype(jnp.float32)
-    chem_pot = lookup(mu_table, rung_mu[0])
-    target = lookup(target_table, rung_mu[0])
-    rho = pore_mask * jnp.exp(chem_pot - potential)
+    group = lax.axis_size("ty") * lax.axis_size("tx")
+    rungs = lax.axis_size("rung")
+    tile = jax.ShapeDtypeStruct(potential.shape, jnp.float32)
+    wide = jax.ShapeDtypeStruct((planes, TALL, WIDE), jnp.float32)
     mats = [jnp.asarray(m) for m in (COLS_FWD, FRONT, BACK, COLS_BACK)]
+    rho_wide = pl.pallas_call(
+        start_kernel,
+        out_shape=wide,
+        in_specs=[VM, VM, SM, SM],
+        out_specs=VM,
+        scratch_shapes=[dma(5), dma(5)],
+        compiler_params=talks(0),
+    )(potential, labels, rung_mu, mu_table)
     weight, dens = pl.pallas_call(
         functools.partial(first_kernel, planes),
-        out_shape=(
-            jax.ShapeDtypeStruct(potential.shape, jnp.float32),
-            jax.ShapeDtypeStruct((planes, 5 * MID, WIDE), jnp.float32),
-        ),
+        out_shape=(tile, jax.ShapeDtypeStruct((planes, 5 * MID, WIDE), jnp.float32)),
         in_specs=[VM] * 7,
         out_specs=(VM, VM),
         scratch_shapes=scratch(planes),
         compiler_params=PARAMS,
-    )(gather_tiles(rho), potential, labels, *mats)
-    cell_total = weight.size * lax.axis_size("ty") * lax.axis_size("tx")
-    amount = lax.psum(jnp.sum(weight), ("ty", "tx")) / cell_total
-    coefficient = jnp.log(amount / target) / amount
+    )(rho_wide, potential, labels, *mats)
+    weight_wide, amounts = pl.pallas_call(
+        weight_kernel,
+        out_shape=(wide, jax.ShapeDtypeStruct((ROWS, LANES), jnp.float32)),
+        in_specs=[VM],
+        out_specs=(VM, VM),
+        scratch_shapes=[
+            pltpu.VMEM((group, ROWS, LANES), jnp.float32),
+            dma(5), dma(5), dma(group), dma(group),
+        ],
+        compiler_params=talks(1),
+    )(weight)
     grad = pl.pallas_call(
-        functools.partial(second_kernel, planes),
-        out_shape=jax.ShapeDtypeStruct(potential.shape, jnp.float32),
-        in_specs=[VM] * 3 + [SM] + [VM] * 4,
+        functools.partial(second_kernel, planes, potential.size * group),
+        out_shape=tile,
+        in_specs=[VM] * 4 + [SM] * 2 + [VM] * 4,
         out_specs=VM,
         scratch_shapes=scratch(planes),
         compiler_params=PARAMS,
-    )(gather_tiles(weight), dens, rho, coefficient[None], *mats)
-    return lax.psum(grad, "rung")
+    )(weight_wide, dens, rho_wide, amounts, rung_mu, target_table, *mats)
+    return pl.pallas_call(
+        rung_kernel,
+        out_shape=tile,
+        in_specs=[VM],
+        out_specs=VM,
+        scratch_shapes=[
+            pltpu.VMEM((rungs - 1,) + potential.shape, jnp.float32),
+            dma(rungs - 1), dma(rungs - 1),
+        ],
+        compiler_params=talks(2),
+    )(grad)
 
 
 def solution(mesh):

time: 118 us -> 75.1 us (0.64)
  waiting for transfers between devices: 32.9 us -> 0 us
  Pallas kernels: 35.4 us -> 66.9 us
  blocking collectives: 15.9 us -> 0 us
  between operations: 15.5 us -> 0.71 us
  starting transfers between devices: 9.07 us -> 0 us
  other arithmetic: 7.05 us -> 0 us
  local copies, waits for them, and re-layouts: 1.6 us -> 7.29 us
    pallas_call x2 -> x5, Pallas kernels: 35.4 us -> 66.9 us  [the longest x1 18.4 us: body(): pl.pallas_call(functools.partial(second_kernel, planes, potential.size *...]
    psum x1 -> x0, waiting for transfers between devices: 19.9 us -> none  [body(): return lax.psum(grad, 'rung')]
    psum x1 -> x0, blocking collectives: 15.9 us -> none  [body(): amount = lax.psum(jnp.sum(weight), ('ty', 'tx')) / cell_total]
    ppermute x6 -> x0, waiting for transfers between devices: 13.1 us -> none  [the longest x2 7.45 us: gather_tiles(): above = lax.ppermute(tile, 'ty', ahead)]
    ppermute x6 -> x0, starting transfers between devices: 9.07 us -> none  [the longest x2 7.6 us: gather_tiles(): below = lax.ppermute(tile, 'ty', [(j, i) for i, j in ahead])]
    unnamed x6 -> x17, local copies, waits for them, and re-layouts: 1.59 us -> 7.29 us
    reduce_sum x3 -> x0, other arithmetic: 3.48 us -> none  [the longest x2 1.93 us: lookup(): jnp.sum(jnp.where(jnp.arange(table_vals.shape[0]) == chosen, table_vals,...]
    concatenate x3 -> x0, other arithmetic: 1.93 us -> none  [the longest x2 1.89 us: gather_tiles(): return jnp.concatenate([tall, other], axis=2)]
  transfers between devices with their start and end apart: 7 -> 0, of which waited for: 5 -> 0; matrix products, arithmetic and copies ran while one was open for 2% -> 0% of each run, Pallas kernels for 0% -> 0%
where the time goes in v2:
time: 75.1 us; the launch traced here: 74.9 us
  Pallas kernels  66.9 us (89%)
  local copies, waits for them, and re-layouts  7.29 us (10%)
    pallas_call x1, Pallas kernels, body(): pl.pallas_call(functools.partial(second_kernel, planes, potential.size *...  18.4 us
    pallas_call x1, Pallas kernels, body(): pl.pallas_call(functools.partial(first_kernel, planes), out_shape=(tile,...  17.2 us
    pallas_call x1, Pallas kernels, body(): pl.pallas_call(weight_kernel, out_shape=(wide, jax.ShapeDtypeStruct((ROWS...  13.2 us
    pallas_call x1, Pallas kernels, body(): pl.pallas_call(start_kernel, out_shape=wide, in_specs=[VM, VM, SM, SM], o...  12.3 us
    unnamed x17, local copies, waits for them, and re-layouts  7.29 us
    pallas_call x1, Pallas kernels, body(): pl.pallas_call(rung_kernel, out_shape=tile, in_specs=[VM], out_specs=VM,...  5.77 us

profile of v2, /device:TPU:0, one launch (start us, length us, event | category | flops | bytes accessed | tf_op | source)
XLA Modules:
  0.0 74.9 jit_solution(14835723753901935427)
XLA Ops:
  0.7 0.0 copy-start.2
  0.7 0.9 %copy-done.2 = f32[32,8,128]{2,1,0:T(8,128)S(1)} copy-done((f32[32,8,128]{2,1,0:T(8,128)S(1)}, f32[32,8,128]{2,1,0:T(8,128)}, u32[]{:S(2)}) %copy-start.2) | copy-done | bytes 131096
  1.6 0.0 copy-start.3
  1.6 0.9 %copy-done.3 = s32[32,8,128]{2,1,0:T(8,128)S(1)} copy-done((s32[32,8,128]{2,1,0:T(8,128)S(1)}, s32[32,8,128]{2,1,0:T(8,128)}, u32[]{:S(2)}) %copy-start.3) | copy-done | bytes 131096
  2.5 0.0 copy-start.7
  2.5 0.7 copy-done.7
  3.1 12.3 %shard_map.91.x_ref.rho_ref = f32[32,24,256]{2,1,0:T(8,128)S(1)} custom-call(f32[32,8,128]{2,1,0:T(8,128)S(1)} %copy-done.2, s32[32,8,128]{2,1,0:T(8,128)S(1)} %copy-done.3, s32[1]{0:T(128)S(6)} %copy.11.rung_ref, f32[8]{0:T(128)S(1)} %copy-done.7), custom_call_target="tpu_custom_call" | custom-call | tf_op jit(solution)/shard_map/pallas_call | solution.py:437
  15.4 0.0 copy-start
  15.4 0.9 %copy-done = f32[32,24,256]{2,1,0:T(8,128)} copy-done((f32[32,24,256]{2,1,0:T(8,128)}, f32[32,24,256]{2,1,0:T(8,128)S(1)}, u32[]{:S(2)}) %copy-start) | copy-done | bytes 786456
  16.3 17.2 %shard_map.92 = (f32[32,8,128]{2,1,0:T(8,128)}, f32[32,80,256]{2,1,0:T(8,128)}) custom-call(f32[32,24,256]{2,1,0:T(8,128)} %copy-done, f32[32,8,128]{2,1,0:T(8,128)} %pot_ref.3, s32[32,8,128]{2,1,0:T(8,128)} %lab_ref.3, bf16[256,2048]{1,0:T(8,128)(2,1)} %constant.8.clone.cols_ref, bf16[320,448]{1,0:T(8,128)(2,1)} %constant.9.clone.front_ref, ...), custom_call_target="tpu_custom_call" | custom-call | tf_op jit(solution)/shard_map/pallas_call | solution.py:445
  33.5 0.0 copy-start.5
  33.5 0.9 %copy-done.5 = f32[32,8,128]{2,1,0:T(8,128)S(1)} copy-done((f32[32,8,128]{2,1,0:T(8,128)S(1)}, f32[32,8,128]{2,1,0:T(8,128)}, u32[]{:S(2)}) %copy-start.5) | copy-done | bytes 131096
  34.4 13.2 %shard_map.93 = (f32[32,24,256]{2,1,0:T(8,128)S(1)}, f32[8,128]{1,0:T(8,128)S(1)}) custom-call(f32[32,8,128]{2,1,0:T(8,128)S(1)} %copy-done.5), custom_call_target="tpu_custom_call" | custom-call | tf_op jit(solution)/shard_map/pallas_call | solution.py:453
  47.7 0.0 copy-start.1
  47.7 0.9 %copy-done.1 = f32[32,24,256]{2,1,0:T(8,128)} copy-done((f32[32,24,256]{2,1,0:T(8,128)}, f32[32,24,256]{2,1,0:T(8,128)S(1)}, u32[]{:S(2)}) %copy-start.1) | copy-done | bytes 786456
  48.6 0.0 copy-start.6
  48.6 0.6 copy-done.6
  49.2 18.4 %shard_map.94.grad_ref = f32[32,8,128]{2,1,0:T(8,128)} custom-call(f32[32,24,256]{2,1,0:T(8,128)} %copy-done.1, f32[32,80,256]{2,1,0:T(8,128)} %get-tuple-element.11.dens_ref, f32[32,24,256]{2,1,0:T(8,128)} %copy-done, f32[8,128]{1,0:T(8,128)} %copy-done.6, s32[1]{0:T(128)S(6)} %copy.11.rung_ref, f32[8]{0:T(128)} %table_ref.3, ...), custom_call_target="tpu_custom_call" | custom-call | tf_op jit(solution)/shard_map/pallas_call | solution.py:464
  67.5 0.0 copy-start.4
  67.5 0.9 %copy-done.4 = f32[32,8,128]{2,1,0:T(8,128)S(1)} copy-done((f32[32,8,128]{2,1,0:T(8,128)S(1)}, f32[32,8,128]{2,1,0:T(8,128)}, u32[]{:S(2)}) %copy-start.4) | copy-done | bytes 131096
  68.4 5.8 %shard_map.95 = f32[32,8,128]{2,1,0:T(8,128)S(1)} custom-call(f32[32,8,128]{2,1,0:T(8,128)S(1)} %copy-done.4), custom_call_target="tpu_custom_call" | custom-call | tf_op jit(solution)/shard_map/pallas_call | solution.py:472
  74.2 0.7 copy.12
Async XLA Ops:
  0.7 0.9 %copy-start.2 = (f32[32,8,128]{2,1,0:T(8,128)S(1)}, f32[32,8,128]{2,1,0:T(8,128)}, u32[]{:S(2)}) copy-start(f32[32,8,128]{2,1,0:T(8,128)} %pot_ref.3) | copy-start | bytes 393220
  1.6 0.9 %copy-start.3 = (s32[32,8,128]{2,1,0:T(8,128)S(1)}, s32[32,8,128]{2,1,0:T(8,128)}, u32[]{:S(2)}) copy-start(s32[32,8,128]{2,1,0:T(8,128)} %lab_ref.3) | copy-start | bytes 393220
  2.5 0.7 copy-start.7
  15.4 0.9 %copy-start = (f32[32,24,256]{2,1,0:T(8,128)}, f32[32,24,256]{2,1,0:T(8,128)S(1)}, u32[]{:S(2)}) copy-start(f32[32,24,256]{2,1,0:T(8,128)S(1)} %shard_map.91.x_ref.rho_ref) | copy-start | bytes 2359300
  33.5 0.9 %copy-start.5 = (f32[32,8,128]{2,1,0:T(8,128)S(1)}, f32[32,8,128]{2,1,0:T(8,128)}, u32[]{:S(2)}) copy-start(f32[32,8,128]{2,1,0:T(8,128)} %get-tuple-element.9.weight_ref) | copy-start | bytes 393220
  47.7 0.9 %copy-start.1 = (f32[32,24,256]{2,1,0:T(8,128)}, f32[32,24,256]{2,1,0:T(8,128)S(1)}, u32[]{:S(2)}) copy-start(f32[32,24,256]{2,1,0:T(8,128)S(1)} %get-tuple-element.10.x_ref) | copy-start | bytes 2359300
  48.6 0.6 copy-start.6
  67.5 0.9 %copy-start.4 = (f32[32,8,128]{2,1,0:T(8,128)S(1)}, f32[32,8,128]{2,1,0:T(8,128)}, u32[]{:S(2)}) copy-start(f32[32,8,128]{2,1,0:T(8,128)} %shard_map.94.grad_ref) | copy-start | bytes 393220

commit v3 on v2

--- a/solution.py
+++ b/solution.py
@@ -19,6 +19,8 @@
 WIDE = 256
 KINDS = 2 * RADIUS + 1
 DEPTH = 224
+BOX_IN = (RADIUS + 1) * TALL
+BOX_OUT = 3 * (RADIUS + 1) * MID
 COEF_A = 1.0 / (4.0 * math.pi * RADIUS * RADIUS)
 COEF_B = 1.0 / (4.0 * math.pi * RADIUS)
 COEF_C = 1.0 / (24.0 * math.pi)
@@ -89,7 +91,9 @@
                     if k > 0:
                         mat[3, p, r, (RADIUS + k) * TALL + src] += sign
     flat = mat.reshape(4 * (RADIUS + 1) * MID, DEPTH)
-    return np.concatenate([flat, flat], axis=1)
+    box = flat[:BOX_OUT, :BOX_IN]
+    moment = flat[BOX_OUT:, BOX_IN : KINDS * TALL]
+    return np.concatenate([box, box], axis=1), np.concatenate([moment, moment], axis=1)
 
 
 def collect_rows():
@@ -118,7 +122,7 @@
 BF = ml_dtypes.bfloat16
 COLS_FWD = np.concatenate([COLS[k] for k in range(1, KINDS)], axis=1).astype(BF)
 COLS_BACK = np.concatenate([COLS[k][:, :LANES] for k in range(KINDS)], axis=0).astype(BF)
-FRONT = spread_rows().astype(BF)
+FRONT_BOX, FRONT_MOM = [m.astype(BF) for m in spread_rows()]
 BACK = BACK.astype(BF)
 N_BACK = len(USED) * ROWS
 
@@ -142,7 +146,12 @@
         c_ref[:, k * WIDE : (k + 1) * WIDE] = dot(high, mat) + dot(low, mat)
 
 
-def rows_forward(planes, c_ref, front_ref, y_ref):
+def stack_parts(x):
+    high = x.astype(jnp.bfloat16).astype(jnp.float32)
+    return jnp.concatenate([high, x - high], axis=0).astype(jnp.bfloat16)
+
+
+def rows_forward(planes, c_ref, box_ref, mom_ref, y_ref):
     zeros = jnp.zeros((RADIUS, GROUPS * MID, WIDE), jnp.float32)
     y_ref[0:RADIUS] = zeros
     y_ref[RADIUS + planes :] = zeros
@@ -150,9 +159,10 @@
     def step(q, carry):
         start = pl.multiple_of(q * TALL, TALL)
         parts = [c_ref[pl.ds(start, TALL), k * WIDE : (k + 1) * WIDE] for k in range(KINDS)]
-        parts.append(jnp.zeros((DEPTH - KINDS * TALL, WIDE), jnp.float32))
-        high, low = split(jnp.concatenate(parts, axis=0))
-        y_ref[q + RADIUS] = dot(front_ref[...], jnp.concatenate([high, low], axis=0))
+        boxes = jnp.concatenate(parts[: RADIUS + 1], axis=0)
+        moments = jnp.concatenate(parts[RADIUS + 1 :], axis=0)
+        y_ref[q + RADIUS, 0:BOX_OUT, :] = dot(box_ref[...], stack_parts(boxes))
+        y_ref[q + RADIUS, BOX_OUT:, :] = dot(mom_ref[...], stack_parts(moments))
         return carry
 
     lax.fori_loop(0, planes, step, 0, unroll=4)
@@ -246,11 +256,11 @@
 
 
 def first_kernel(
-    planes, x_ref, pot_ref, lab_ref, cols_ref, front_ref, back_ref, colsb_ref,
+    planes, x_ref, pot_ref, lab_ref, cols_ref, box_ref, mom_ref, back_ref, colsb_ref,
     weight_ref, dens_ref, c_ref, y_ref, z_ref, d_ref,
 ):
     columns_forward(planes, x_ref, cols_ref, c_ref)
-    rows_forward(planes, c_ref, front_ref, y_ref)
+    rows_forward(planes, c_ref, box_ref, mom_ref, y_ref)
     clear_edges(planes, z_ref)
 
     def step(q, carry):
@@ -267,11 +277,11 @@
 
 
 def second_kernel(
-    planes, cells, x_ref, dens_ref, rho_ref, sum_ref, rung_ref, table_ref, cols_ref, front_ref, back_ref, colsb_ref,
+    planes, cells, x_ref, dens_ref, rho_ref, sum_ref, rung_ref, table_ref, cols_ref, box_ref, mom_ref, back_ref, colsb_ref,
     out_ref, c_ref, y_ref, z_ref, d_ref,
 ):
     columns_forward(planes, x_ref, cols_ref, c_ref)
-    rows_forward(planes, c_ref, front_ref, y_ref)
+    rows_forward(planes, c_ref, box_ref, mom_ref, y_ref)
     clear_edges(planes, z_ref)
 
     def step(q, carry):
@@ -299,7 +309,8 @@
     ]
 
 
-PARAMS = pltpu.CompilerParams(vmem_limit_bytes=58 * 1024 * 1024)
+PARAMS = pltpu.CompilerParams(vmem_limit_bytes=47 * 1024 * 1024)
+COST = pl.CostEstimate(flops=5_000_000_000, bytes_accessed=30_000_000, transcendentals=0)
 VM = pl.BlockSpec(memory_space=pltpu.VMEM)
 SM = pl.BlockSpec(memory_space=pltpu.SMEM)
 
@@ -419,7 +430,7 @@
 
 def talks(place):
     return pltpu.CompilerParams(
-        collective_id=place, has_side_effects=True, vmem_limit_bytes=24 * 1024 * 1024
+        collective_id=place, has_side_effects=True, vmem_limit_bytes=8 * 1024 * 1024
     )
 
 
@@ -433,7 +444,7 @@
     rungs = lax.axis_size("rung")
     tile = jax.ShapeDtypeStruct(potential.shape, jnp.float32)
     wide = jax.ShapeDtypeStruct((planes, TALL, WIDE), jnp.float32)
-    mats = [jnp.asarray(m) for m in (COLS_FWD, FRONT, BACK, COLS_BACK)]
+    mats = [jnp.asarray(m) for m in (COLS_FWD, FRONT_BOX, FRONT_MOM, BACK, COLS_BACK)]
     rho_wide = pl.pallas_call(
         start_kernel,
         out_shape=wide,
@@ -441,14 +452,16 @@
         out_specs=VM,
         scratch_shapes=[dma(5), dma(5)],
         compiler_params=talks(0),
+        cost_estimate=COST,
     )(potential, labels, rung_mu, mu_table)
     weight, dens = pl.pallas_call(
         functools.partial(first_kernel, planes),
         out_shape=(tile, jax.ShapeDtypeStruct((planes, 5 * MID, WIDE), jnp.float32)),
-        in_specs=[VM] * 7,
+        in_specs=[VM] * 8,
         out_specs=(VM, VM),
         scratch_shapes=scratch(planes),
         compiler_params=PARAMS,
+        cost_estimate=COST,
     )(rho_wide, potential, labels, *mats)
     weight_wide, amounts = pl.pallas_call(
         weight_kernel,
@@ -460,14 +473,16 @@
             dma(5), dma(5), dma(group), dma(group),
         ],
         compiler_params=talks(1),
+        cost_estimate=COST,
     )(weight)
     grad = pl.pallas_call(
         functools.partial(second_kernel, planes, potential.size * group),
         out_shape=tile,
-        in_specs=[VM] * 4 + [SM] * 2 + [VM] * 4,
+        in_specs=[VM] * 4 + [SM] * 2 + [VM] * 5,
         out_specs=VM,
         scratch_shapes=scratch(planes),
         compiler_params=PARAMS,
+        cost_estimate=COST,
     )(weight_wide, dens, rho_wide, amounts, rung_mu, target_table, *mats)
     return pl.pallas_call(
         rung_kernel,
@@ -479,6 +494,7 @@
             dma(rungs - 1), dma(rungs - 1),
         ],
         compiler_params=talks(2),
+        cost_estimate=COST,
     )(grad)
 
 

time: 75.1 us -> 62.6 us (0.83)
  Pallas kernels: 66.9 us -> 58.5 us
  local copies, waits for them, and re-layouts: 7.29 us -> 3.16 us
    pallas_call x1, Pallas kernels: 18.4 us -> 14 us  [body(): pl.pallas_call(functools.partial(second_kernel, planes, potential.size *...]
    pallas_call x1, Pallas kernels: 17.2 us -> 13.1 us  [body(): pl.pallas_call(functools.partial(first_kernel, planes), out_shape=(tile,...]
    unnamed x17 -> x23, local copies, waits for them, and re-layouts: 7.29 us -> 3.16 us
where the time goes in v3:
time: 62.6 us; the launch traced here: 62.5 us
  Pallas kernels  58.5 us (93%)
  local copies, waits for them, and re-layouts  3.16 us (5%)
  between operations  0.8 us (1%)
    pallas_call x1, Pallas kernels, body(): pl.pallas_call(functools.partial(second_kernel, planes, potential.size *...  14 us
    pallas_call x1, Pallas kernels, body(): pl.pallas_call(weight_kernel, out_shape=(wide, jax.ShapeDtypeStruct((ROWS...  13.3 us
    pallas_call x1, Pallas kernels, body(): pl.pallas_call(functools.partial(first_kernel, planes), out_shape=(tile,...  13.1 us
    pallas_call x1, Pallas kernels, body(): pl.pallas_call(start_kernel, out_shape=wide, in_specs=[VM, VM, SM, SM], o...  12.3 us
    pallas_call x1, Pallas kernels, body(): pl.pallas_call(rung_kernel, out_shape=tile, in_specs=[VM], out_specs=VM,...  5.83 us
    unnamed x23, local copies, waits for them, and re-layouts  3.16 us

profile of v3, /device:TPU:0, one launch (start us, length us, event | category | flops | bytes accessed | tf_op | source)
XLA Modules:
  0.0 62.5 jit_solution(11966633593699100669)
XLA Ops:
  0.7 0.0 copy-start
  0.7 0.9 %copy-done = f32[32,8,128]{2,1,0:T(8,128)S(1)} copy-done((f32[32,8,128]{2,1,0:T(8,128)S(1)}, f32[32,8,128]{2,1,0:T(8,128)}, u32[]{:S(2)}) %copy-start) | copy-done | bytes 131096
  1.6 0.0 copy-start.2
  1.6 0.9 %copy-done.2 = s32[32,8,128]{2,1,0:T(8,128)S(1)} copy-done((s32[32,8,128]{2,1,0:T(8,128)S(1)}, s32[32,8,128]{2,1,0:T(8,128)}, u32[]{:S(2)}) %copy-start.2) | copy-done | bytes 131096
  2.5 0.0 copy-start.4
  2.5 0.7 %copy-done.4 = f32[8]{0:T(128)S(1)} copy-done((f32[8]{0:T(128)S(1)}, f32[8]{0:T(128)}, u32[]{:S(2)}) %copy-start.4) | copy-done | bytes 56
  3.1 0.0 copy-start.1
  3.1 0.0 copy-start.3
  3.1 0.0 copy-start.6
  3.1 0.0 copy-start.7
  3.1 0.0 copy-start.8
  3.1 0.0 copy-start.9
  3.2 0.0 copy-start.10
  3.2 12.3 %shard_map.100.x_ref.rho_ref = f32[32,24,256]{2,1,0:T(8,128)S(1)} custom-call(f32[32,8,128]{2,1,0:T(8,128)S(1)} %copy-done, s32[32,8,128]{2,1,0:T(8,128)S(1)} %copy-done.2, s32[1]{0:T(128)S(6)} %copy.12.rung_ref, f32[8]{0:T(128)S(1)} %copy-done.4), custom_call_target="tpu_custom_call" | custom-call | flops 5000000000 | bytes 30000000 | tf_op jit(solution)/shard_map/pallas_call | solution.py:448
  15.5 0.0 copy-done.1
  15.5 0.0 copy-done.3
  15.5 0.0 copy-done.6
  15.5 0.0 copy-done.7
  15.5 0.0 copy-done.8
  15.5 0.0 copy-done.9
  15.5 0.0 copy-done.10
  15.6 13.1 %shard_map.101 = (f32[32,8,128]{2,1,0:T(8,128)S(1)}, f32[32,80,256]{2,1,0:T(8,128)S(1)}) custom-call(f32[32,24,256]{2,1,0:T(8,128)S(1)} %shard_map.100.x_ref.rho_ref, f32[32,8,128]{2,1,0:T(8,128)S(1)} %copy-done.1, s32[32,8,128]{2,1,0:T(8,128)S(1)} %copy-done.3, bf16[256,2048]{1,0:T(8,128)(2,1)S(1)} %copy-done.6, bf16[240,240]{1,0:T(8,128)(2,1)S(1)} %copy-done.9, ...), custom_call_target="tpu_custom_call" | custom-call | flops 5000000000 | bytes 30000000 | tf_op jit(solution)/shard_map/pallas_call | solution.py:457
  28.6 0.0 copy-start.5
  28.6 13.3 %shard_map.102 = (f32[32,24,256]{2,1,0:T(8,128)S(1)}, f32[8,128]{1,0:T(8,128)S(1)}) custom-call(f32[32,8,128]{2,1,0:T(8,128)S(1)} %get-tuple-element.9.weight_ref), custom_call_target="tpu_custom_call" | custom-call | flops 5000000000 | bytes 30000000 | tf_op jit(solution)/shard_map/pallas_call | solution.py:466
  41.9 0.0 copy-done.5
  41.9 14.0 %shard_map.103.grad_ref = f32[32,8,128]{2,1,0:T(8,128)S(1)} custom-call(f32[32,24,256]{2,1,0:T(8,128)S(1)} %get-tuple-element.10.x_ref, f32[32,80,256]{2,1,0:T(8,128)S(1)} %get-tuple-element.11.dens_ref, f32[32,24,256]{2,1,0:T(8,128)S(1)} %shard_map.100.x_ref.rho_ref, f32[8,128]{1,0:T(8,128)S(1)} %get-tuple-element.12.sum_ref, s32[1]{0:T(128)S(6)} %copy.12.rung_ref, ...), custom_call_target="tpu_custom_call" | custom-call | flops 5000000000 | bytes 30000000 | tf_op jit(solution)/shard_map/pallas_call | solution.py:478
  56.0 5.8 %shard_map.104 = f32[32,8,128]{2,1,0:T(8,128)S(1)} custom-call(f32[32,8,128]{2,1,0:T(8,128)S(1)} %shard_map.103.grad_ref), custom_call_target="tpu_custom_call" | custom-call | flops 5000000000 | bytes 30000000 | tf_op jit(solution)/shard_map/pallas_call | solution.py:487
  61.8 0.7 %copy.13 = f32[32,8,128]{2,1,0:T(8,128)} copy(f32[32,8,128]{2,1,0:T(8,128)S(1)} %shard_map.104) | data formatting | bytes 262144
Async XLA Ops:
  0.7 0.9 %copy-start = (f32[32,8,128]{2,1,0:T(8,128)S(1)}, f32[32,8,128]{2,1,0:T(8,128)}, u32[]{:S(2)}) copy-start(f32[32,8,128]{2,1,0:T(8,128)} %pot_ref.3) | copy-start | bytes 393220
  1.6 0.9 %copy-start.2 = (s32[32,8,128]{2,1,0:T(8,128)S(1)}, s32[32,8,128]{2,1,0:T(8,128)}, u32[]{:S(2)}) copy-start(s32[32,8,128]{2,1,0:T(8,128)} %lab_ref.3) | copy-start | bytes 393220
  2.5 0.7 %copy-start.4 = (f32[8]{0:T(128)S(1)}, f32[8]{0:T(128)}, u32[]{:S(2)}) copy-start(f32[8]{0:T(128)} %table_ref.2) | copy-start | bytes 100
  3.1 12.4 %copy-start.1 = (f32[32,8,128]{2,1,0:T(8,128)S(1)}, f32[32,8,128]{2,1,0:T(8,128)}, u32[]{:S(2)}) copy-start(f32[32,8,128]{2,1,0:T(8,128)} %pot_ref.3) | copy-start | bytes 393220
  3.1 12.4 %copy-start.3 = (s32[32,8,128]{2,1,0:T(8,128)S(1)}, s32[32,8,128]{2,1,0:T(8,128)}, u32[]{:S(2)}) copy-start(s32[32,8,128]{2,1,0:T(8,128)} %lab_ref.3) | copy-start | bytes 393220
  3.1 12.4 %copy-start.6 = (bf16[256,2048]{1,0:T(8,128)(2,1)S(1)}, bf16[256,2048]{1,0:T(8,128)(2,1)}, u32[]{:S(2)}) copy-start(bf16[256,2048]{1,0:T(8,128)(2,1)} %constant.10.clone.cols_ref) | copy-start | bytes 3145732
  3.1 12.4 %copy-start.7 = (bf16[2304,128]{1,0:T(8,128)(2,1)S(1)}, bf16[2304,128]{1,0:T(8,128)(2,1)}, u32[]{:S(2)}) copy-start(bf16[2304,128]{1,0:T(8,128)(2,1)} %constant.14.clone.colsb_ref) | copy-start | bytes 1769476
  3.1 12.4 %copy-start.8 = (bf16[504,160]{1,0:T(8,128)(2,1)S(1)}, bf16[504,160]{1,0:T(8,128)(2,1)}, u32[]{:S(2)}) copy-start(bf16[504,160]{1,0:T(8,128)(2,1)} %constant.13.clone.back_ref) | copy-start | bytes 483844
  3.1 12.4 %copy-start.9 = (bf16[240,240]{1,0:T(8,128)(2,1)S(1)}, bf16[240,240]{1,0:T(8,128)(2,1)}, u32[]{:S(2)}) copy-start(bf16[240,240]{1,0:T(8,128)(2,1)} %constant.11.clone.box_ref) | copy-start | bytes 345604
  3.2 12.4 %copy-start.10 = (bf16[80,192]{1,0:T(8,128)(2,1)S(1)}, bf16[80,192]{1,0:T(8,128)(2,1)}, u32[]{:S(2)}) copy-start(bf16[80,192]{1,0:T(8,128)(2,1)} %constant.12.clone.mom_ref) | copy-start | bytes 92164
  28.6 13.3 %copy-start.5 = (f32[8]{0:T(128)S(1)}, f32[8]{0:T(128)}, u32[]{:S(2)}) copy-start(f32[8]{0:T(128)} %table_ref.3) | copy-start | bytes 100

commit v4 on v3

--- a/solution.py
+++ b/solution.py
@@ -138,7 +138,8 @@
 
 
 def columns_forward(planes, x_ref, cols_ref, c_ref):
-    x = x_ref[...].reshape(planes * TALL, WIDE)
+    strips = [jnp.concatenate([x_ref[b], x_ref[b + 1]], axis=2) for b in (0, 2, 4)]
+    x = jnp.concatenate(strips, axis=1).reshape(planes * TALL, WIDE)
     c_ref[:, 0:WIDE] = x
     high, low = split(x)
     for k in range(1, KINDS):
@@ -292,8 +293,8 @@
 
     lax.fori_loop(0, planes, step, 0, unroll=2)
     total = columns_back(planes, z_ref, colsb_ref, d_ref)
-    weight = x_ref[:, ROWS : 2 * ROWS, 0:LANES]
-    rho = rho_ref[:, ROWS : 2 * ROWS, 0:LANES]
+    weight = x_ref[2]
+    rho = rho_ref[2]
     amount = jnp.sum(sum_ref[...], axis=(0, 1), keepdims=True) * (1.0 / cells)
     amount = jnp.broadcast_to(amount, (ROWS, LANES))
     coefficient = jnp.log(amount / pick(rung_ref[0], table_ref)) / amount
@@ -316,6 +317,7 @@
 
 
 MESH = pl.DeviceIdType.MESH
+CHUNKS = 2
 
 
 def pick(index, table_ref):
@@ -328,33 +330,39 @@
 def swap_tiles(x_ref, send_sem, recv_sem):
     count = lax.axis_size("ty")
     ty, tx = lax.axis_index("ty"), lax.axis_index("tx")
-    own = x_ref.at[:, ROWS : 2 * ROWS, 0:LANES]
-
-    def copy(i, src, rows, lane, device):
-        dst = x_ref.at[:, rows : rows + ROWS, lane : lane + LANES]
+    size = x_ref.shape[1] // CHUNKS
+
+    def copy(i, chunk, src, dst, device):
+        place = pl.ds(chunk * size, size)
         return pltpu.make_async_remote_copy(
-            src_ref=src, dst_ref=dst, send_sem=send_sem.at[i], recv_sem=recv_sem.at[i],
+            src_ref=x_ref.at[src, place], dst_ref=x_ref.at[dst, place],
+            send_sem=send_sem.at[i * CHUNKS + chunk], recv_sem=recv_sem.at[i * CHUNKS + chunk],
             device_id=device, device_id_type=MESH,
         )
 
+    chunks = range(CHUNKS)
     beside = {"tx": 1 - tx}
-    down = copy(0, own, 0, 0, {"ty": lax.rem(ty + 1, count)})
-    up = copy(1, own, 2 * ROWS, 0, {"ty": lax.rem(ty + count - 1, count)})
-    side = copy(2, own, ROWS, LANES, beside)
-    down.start()
-    up.start()
-    side.start()
-    head = copy(3, x_ref.at[:, 0:ROWS, 0:LANES], 0, LANES, beside)
-    tail = copy(4, x_ref.at[:, 2 * ROWS : 3 * ROWS, 0:LANES], 2 * ROWS, LANES, beside)
-    down.wait_recv()
-    head.start()
-    up.wait_recv()
-    tail.start()
-    down.wait_send()
-    up.wait_send()
-    side.wait()
-    head.wait()
-    tail.wait()
+    down = [copy(0, c, 2, 0, {"ty": lax.rem(ty + 1, count)}) for c in chunks]
+    up = [copy(1, c, 2, 4, {"ty": lax.rem(ty + count - 1, count)}) for c in chunks]
+    side = [copy(2, c, 2, 3, beside) for c in chunks]
+    head = [copy(3, c, 0, 1, beside) for c in chunks]
+    tail = [copy(4, c, 4, 5, beside) for c in chunks]
+    for c in chunks:
+        down[c].start()
+        up[c].start()
+    for c in chunks:
+        side[c].start()
+    for c in chunks:
+        down[c].wait_recv()
+        head[c].start()
+        up[c].wait_recv()
+        tail[c].start()
+    for c in chunks:
+        down[c].wait_send()
+        up[c].wait_send()
+        side[c].wait()
+        head[c].wait()
+        tail[c].wait()
 
 
 def greet(devices):
@@ -364,15 +372,17 @@
     pl.semaphore_wait(barrier, len(devices))
 
 
-def start_kernel(pot_ref, lab_ref, rung_ref, table_ref, x_ref, send_sem, recv_sem):
+def start_kernel(
+    pot_ref, lab_ref, rung_ref, table_ref, x_ref, send_sem, recv_sem,
+):
     count = lax.axis_size("ty")
     ty, tx = lax.axis_index("ty"), lax.axis_index("tx")
-    chem_pot = pick(rung_ref[0], table_ref)
-    mask = lab_ref[...].astype(jnp.float32)
-    x_ref[:, ROWS : 2 * ROWS, 0:LANES] = mask * jnp.exp(chem_pot - pot_ref[...])
     greet([
         {"ty": lax.rem(ty + 1, count)}, {"ty": lax.rem(ty + count - 1, count)}, {"tx": 1 - tx},
     ])
+    chem_pot = pick(rung_ref[0], table_ref)
+    mask = lab_ref[...].astype(jnp.float32)
+    x_ref[2] = mask * jnp.exp(chem_pot - pot_ref[...])
     swap_tiles(x_ref, send_sem, recv_sem)
 
 
@@ -387,7 +397,7 @@
         target = lax.rem(me + j, group)
         others.append({"ty": target // cores, "tx": lax.rem(target, cores)})
     weight = weight_ref[...]
-    x_ref[:, ROWS : 2 * ROWS, 0:LANES] = weight
+    x_ref[2] = weight
     slots[0] = jnp.sum(weight, axis=0)
     greet(others)
     copies = []
@@ -443,14 +453,16 @@
     group = lax.axis_size("ty") * lax.axis_size("tx")
     rungs = lax.axis_size("rung")
     tile = jax.ShapeDtypeStruct(potential.shape, jnp.float32)
-    wide = jax.ShapeDtypeStruct((planes, TALL, WIDE), jnp.float32)
+    wide = jax.ShapeDtypeStruct((6,) + potential.shape, jnp.float32)
     mats = [jnp.asarray(m) for m in (COLS_FWD, FRONT_BOX, FRONT_MOM, BACK, COLS_BACK)]
     rho_wide = pl.pallas_call(
         start_kernel,
         out_shape=wide,
         in_specs=[VM, VM, SM, SM],
         out_specs=VM,
-        scratch_shapes=[dma(5), dma(5)],
+        scratch_shapes=[
+            dma(5 * CHUNKS), dma(5 * CHUNKS),
+        ],
         compiler_params=talks(0),
         cost_estimate=COST,
     )(potential, labels, rung_mu, mu_table)
@@ -470,7 +482,7 @@
         out_specs=(VM, VM),
         scratch_shapes=[
             pltpu.VMEM((group, ROWS, LANES), jnp.float32),
-            dma(5), dma(5), dma(group), dma(group),
+            dma(5 * CHUNKS), dma(5 * CHUNKS), dma(group), dma(group),
         ],
         compiler_params=talks(1),
         cost_estimate=COST,

time: 62.6 us -> 62.6 us (level)
    pallas_call x1, Pallas kernels: 12.3 us -> 13 us  [body(): pl.pallas_call(start_kernel, out_shape=wide, in_specs=[VM, VM, SM, SM], o...]
    pallas_call x1, Pallas kernels: 13.3 us -> 12.6 us  [body(): pl.pallas_call(weight_kernel, out_shape=(wide, jax.ShapeDtypeStruct((ROWS...]
where the time goes in v4:
time: 62.6 us; the launch traced here: 62.5 us
  Pallas kernels  58.5 us (93%)
  local copies, waits for them, and re-layouts  3.16 us (5%)
  between operations  0.8 us (1%)
    pallas_call x1, Pallas kernels, body(): pl.pallas_call(functools.partial(second_kernel, planes, potential.size *...  14 us
    pallas_call x1, Pallas kernels, body(): pl.pallas_call(functools.partial(first_kernel, planes), out_shape=(tile,...  13.1 us
    pallas_call x1, Pallas kernels, body(): pl.pallas_call(start_kernel, out_shape=wide, in_specs=[VM, VM, SM, SM], o...  13 us
    pallas_call x1, Pallas kernels, body(): pl.pallas_call(weight_kernel, out_shape=(wide, jax.ShapeDtypeStruct((ROWS...  12.6 us
    pallas_call x1, Pallas kernels, body(): pl.pallas_call(rung_kernel, out_shape=tile, in_specs=[VM], out_specs=VM,...  5.82 us
    unnamed x23, local copies, waits for them, and re-layouts  3.16 us

profile of v4, /device:TPU:0, one launch (start us, length us, event | category | flops | bytes accessed | tf_op | source)
XLA Modules:
  0.0 62.5 jit_solution(16001198975733905511)
XLA Ops:
  0.7 0.0 copy-start
  0.7 0.9 %copy-done = f32[32,8,128]{2,1,0:T(8,128)S(1)} copy-done((f32[32,8,128]{2,1,0:T(8,128)S(1)}, f32[32,8,128]{2,1,0:T(8,128)}, u32[]{:S(2)}) %copy-start) | copy-done | bytes 131096
  1.6 0.0 copy-start.2
  1.6 0.9 %copy-done.2 = s32[32,8,128]{2,1,0:T(8,128)S(1)} copy-done((s32[32,8,128]{2,1,0:T(8,128)S(1)}, s32[32,8,128]{2,1,0:T(8,128)}, u32[]{:S(2)}) %copy-start.2) | copy-done | bytes 131096
  2.5 0.0 copy-start.4
  2.5 0.7 %copy-done.4 = f32[8]{0:T(128)S(1)} copy-done((f32[8]{0:T(128)S(1)}, f32[8]{0:T(128)}, u32[]{:S(2)}) %copy-start.4) | copy-done | bytes 56
  3.1 0.0 copy-start.1
  3.1 0.0 copy-start.3
  3.1 0.0 copy-start.6
  3.1 0.0 copy-start.7
  3.1 0.0 copy-start.8
  3.1 0.0 copy-start.9
  3.2 0.0 copy-start.10
  3.2 13.0 %shard_map.100.x_ref.rho_ref = f32[6,32,8,128]{3,2,1,0:T(8,128)S(1)} custom-call(f32[32,8,128]{2,1,0:T(8,128)S(1)} %copy-done, s32[32,8,128]{2,1,0:T(8,128)S(1)} %copy-done.2, s32[1]{0:T(128)S(6)} %copy.12.rung_ref, f32[8]{0:T(128)S(1)} %copy-done.4), custom_call_target="tpu_custom_call" | custom-call | flops 5000000000 | bytes 30000000 | tf_op jit(solution)/shard_map/pallas_call | solution.py:458
  16.1 0.0 copy-done.1
  16.2 0.0 copy-done.3
  16.2 0.0 copy-done.6
  16.2 0.0 copy-done.7
  16.2 0.0 copy-done.8
  16.2 0.0 copy-done.9
  16.2 0.0 copy-done.10
  16.2 13.1 %shard_map.101 = (f32[32,8,128]{2,1,0:T(8,128)S(1)}, f32[32,80,256]{2,1,0:T(8,128)S(1)}) custom-call(f32[6,32,8,128]{3,2,1,0:T(8,128)S(1)} %shard_map.100.x_ref.rho_ref, f32[32,8,128]{2,1,0:T(8,128)S(1)} %copy-done.1, s32[32,8,128]{2,1,0:T(8,128)S(1)} %copy-done.3, bf16[256,2048]{1,0:T(8,128)(2,1)S(1)} %copy-done.6, bf16[240,240]{1,0:T(8,128)(2,1)S(1)} %copy-done.9, ...), custom_call_target="tpu_custom_call" | custom-call | flops 5000000000 | bytes 30000000 | tf_op jit(solution)/shard_map/pallas_call | solution.py:469
  29.3 0.0 copy-start.5
  29.3 12.6 %shard_map.102 = (f32[6,32,8,128]{3,2,1,0:T(8,128)S(1)}, f32[8,128]{1,0:T(8,128)S(1)}) custom-call(f32[32,8,128]{2,1,0:T(8,128)S(1)} %get-tuple-element.9.weight_ref), custom_call_target="tpu_custom_call" | custom-call | flops 5000000000 | bytes 30000000 | tf_op jit(solution)/shard_map/pallas_call | solution.py:478
  41.9 0.0 copy-done.5
  41.9 14.0 %shard_map.103.grad_ref = f32[32,8,128]{2,1,0:T(8,128)S(1)} custom-call(f32[6,32,8,128]{3,2,1,0:T(8,128)S(1)} %get-tuple-element.10.x_ref, f32[32,80,256]{2,1,0:T(8,128)S(1)} %get-tuple-element.11.dens_ref, f32[6,32,8,128]{3,2,1,0:T(8,128)S(1)} %shard_map.100.x_ref.rho_ref, f32[8,128]{1,0:T(8,128)S(1)} %get-tuple-element.12.sum_ref, s32[1]{0:T(128)S(6)} %copy.12.rung_ref, ...), custom_call_target="tpu_custom_call" | custom-call | flops 5000000000 | bytes 30000000 | tf_op jit(solution)/shard_map/pallas_call | solution.py:490
  56.0 5.8 %shard_map.104 = f32[32,8,128]{2,1,0:T(8,128)S(1)} custom-call(f32[32,8,128]{2,1,0:T(8,128)S(1)} %shard_map.103.grad_ref), custom_call_target="tpu_custom_call" | custom-call | flops 5000000000 | bytes 30000000 | tf_op jit(solution)/shard_map/pallas_call | solution.py:499
  61.8 0.7 %copy.13 = f32[32,8,128]{2,1,0:T(8,128)} copy(f32[32,8,128]{2,1,0:T(8,128)S(1)} %shard_map.104) | data formatting | bytes 262144
Async XLA Ops:
  0.7 0.9 %copy-start = (f32[32,8,128]{2,1,0:T(8,128)S(1)}, f32[32,8,128]{2,1,0:T(8,128)}, u32[]{:S(2)}) copy-start(f32[32,8,128]{2,1,0:T(8,128)} %pot_ref.3) | copy-start | bytes 393220
  1.6 0.9 %copy-start.2 = (s32[32,8,128]{2,1,0:T(8,128)S(1)}, s32[32,8,128]{2,1,0:T(8,128)}, u32[]{:S(2)}) copy-start(s32[32,8,128]{2,1,0:T(8,128)} %lab_ref.3) | copy-start | bytes 393220
  2.5 0.7 %copy-start.4 = (f32[8]{0:T(128)S(1)}, f32[8]{0:T(128)}, u32[]{:S(2)}) copy-start(f32[8]{0:T(128)} %table_ref.2) | copy-start | bytes 100
  3.1 13.0 %copy-start.1 = (f32[32,8,128]{2,1,0:T(8,128)S(1)}, f32[32,8,128]{2,1,0:T(8,128)}, u32[]{:S(2)}) copy-start(f32[32,8,128]{2,1,0:T(8,128)} %pot_ref.3) | copy-start | bytes 393220
  3.1 13.0 %copy-start.3 = (s32[32,8,128]{2,1,0:T(8,128)S(1)}, s32[32,8,128]{2,1,0:T(8,128)}, u32[]{:S(2)}) copy-start(s32[32,8,128]{2,1,0:T(8,128)} %lab_ref.3) | copy-start | bytes 393220
  3.1 13.0 %copy-start.6 = (bf16[256,2048]{1,0:T(8,128)(2,1)S(1)}, bf16[256,2048]{1,0:T(8,128)(2,1)}, u32[]{:S(2)}) copy-start(bf16[256,2048]{1,0:T(8,128)(2,1)} %constant.10.clone.cols_ref) | copy-start | bytes 3145732
  3.1 13.1 %copy-start.7 = (bf16[2304,128]{1,0:T(8,128)(2,1)S(1)}, bf16[2304,128]{1,0:T(8,128)(2,1)}, u32[]{:S(2)}) copy-start(bf16[2304,128]{1,0:T(8,128)(2,1)} %constant.14.clone.colsb_ref) | copy-start | bytes 1769476
  3.1 13.1 %copy-start.8 = (bf16[504,160]{1,0:T(8,128)(2,1)S(1)}, bf16[504,160]{1,0:T(8,128)(2,1)}, u32[]{:S(2)}) copy-start(bf16[504,160]{1,0:T(8,128)(2,1)} %constant.13.clone.back_ref) | copy-start | bytes 483844
  3.1 13.1 %copy-start.9 = (bf16[240,240]{1,0:T(8,128)(2,1)S(1)}, bf16[240,240]{1,0:T(8,128)(2,1)}, u32[]{:S(2)}) copy-start(bf16[240,240]{1,0:T(8,128)(2,1)} %constant.11.clone.box_ref) | copy-start | bytes 345604
  3.2 13.1 %copy-start.10 = (bf16[80,192]{1,0:T(8,128)(2,1)S(1)}, bf16[80,192]{1,0:T(8,128)(2,1)}, u32[]{:S(2)}) copy-start(bf16[80,192]{1,0:T(8,128)(2,1)} %constant.12.clone.mom_ref) | copy-start | bytes 92164
  29.3 12.6 %copy-start.5 = (f32[8]{0:T(128)S(1)}, f32[8]{0:T(128)}, u32[]{:S(2)}) copy-start(f32[8]{0:T(128)} %table_ref.3) | copy-start | bytes 100

commit v5 on v3

--- a/solution.py
+++ b/solution.py
@@ -239,7 +239,7 @@
             d_ref[pl.ds(start, ROWS), k * WIDE : (k + 1) * WIDE] = total
         return carry
 
-    lax.fori_loop(0, planes, step, 0, unroll=2)
+    lax.fori_loop(0, planes, step, 0, unroll=4)
     out = None
     for k in range(KINDS):
         high, low = split(d_ref[:, k * WIDE : (k + 1) * WIDE])
@@ -270,7 +270,7 @@
         push_back(q, derivs_of(*dens), back_ref, z_ref)
         return carry
 
-    lax.fori_loop(0, planes, step, 0, unroll=2)
+    lax.fori_loop(0, planes, step, 0, unroll=4)
     total = columns_back(planes, z_ref, colsb_ref, d_ref)
     mask = lab_ref[...].astype(jnp.float32)
     weight_ref[...] = mask * jnp.exp(-total - pot_ref[...])
@@ -290,7 +290,7 @@
         push_back(q, hess_of(dens, images), back_ref, z_ref)
         return carry
 
-    lax.fori_loop(0, planes, step, 0, unroll=2)
+    lax.fori_loop(0, planes, step, 0, unroll=4)
     total = columns_back(planes, z_ref, colsb_ref, d_ref)
     weight = x_ref[:, ROWS : 2 * ROWS, 0:LANES]
     rho = rho_ref[:, ROWS : 2 * ROWS, 0:LANES]

time: 62.6 us -> 58.9 us (0.941)
  Pallas kernels: 58.5 us -> 54.8 us
    pallas_call x1, Pallas kernels: 14 us -> 12.2 us  [body(): pl.pallas_call(functools.partial(second_kernel, planes, potential.size *...]
    pallas_call x1, Pallas kernels: 13.1 us -> 11.3 us  [body(): pl.pallas_call(functools.partial(first_kernel, planes), out_shape=(tile,...]
where the time goes in v5:
time: 58.9 us; the launch traced here: 58.7 us
  Pallas kernels  54.8 us (93%)
  local copies, waits for them, and re-layouts  3.16 us (5%)
  between operations  0.8 us (1%)
    pallas_call x1, Pallas kernels, body(): pl.pallas_call(weight_kernel, out_shape=(wide, jax.ShapeDtypeStruct((ROWS...  13.2 us
    pallas_call x1, Pallas kernels, body(): pl.pallas_call(start_kernel, out_shape=wide, in_specs=[VM, VM, SM, SM], o...  12.3 us
    pallas_call x1, Pallas kernels, body(): pl.pallas_call(functools.partial(second_kernel, planes, potential.size *...  12.2 us
    pallas_call x1, Pallas kernels, body(): pl.pallas_call(functools.partial(first_kernel, planes), out_shape=(tile,...  11.3 us
    pallas_call x1, Pallas kernels, body(): pl.pallas_call(rung_kernel, out_shape=tile, in_specs=[VM], out_specs=VM,...  5.83 us
    unnamed x23, local copies, waits for them, and re-layouts  3.16 us

profile of v5, /device:TPU:0, one launch (start us, length us, event | category | flops | bytes accessed | tf_op | source)
XLA Modules:
  0.0 58.7 jit_solution(15469630239658573026)
XLA Ops:
  0.7 0.0 copy-start
  0.7 0.9 %copy-done = f32[32,8,128]{2,1,0:T(8,128)S(1)} copy-done((f32[32,8,128]{2,1,0:T(8,128)S(1)}, f32[32,8,128]{2,1,0:T(8,128)}, u32[]{:S(2)}) %copy-start) | copy-done | bytes 131096
  1.6 0.0 copy-start.2
  1.6 0.9 %copy-done.2 = s32[32,8,128]{2,1,0:T(8,128)S(1)} copy-done((s32[32,8,128]{2,1,0:T(8,128)S(1)}, s32[32,8,128]{2,1,0:T(8,128)}, u32[]{:S(2)}) %copy-start.2) | copy-done | bytes 131096
  2.5 0.0 copy-start.4
  2.5 0.7 %copy-done.4 = f32[8]{0:T(128)S(1)} copy-done((f32[8]{0:T(128)S(1)}, f32[8]{0:T(128)}, u32[]{:S(2)}) %copy-start.4) | copy-done | bytes 56
  3.1 0.0 copy-start.1
  3.1 0.0 copy-start.3
  3.1 0.0 copy-start.6
  3.1 0.0 copy-start.7
  3.1 0.0 copy-start.8
  3.1 0.0 copy-start.9
  3.2 0.0 copy-start.10
  3.2 12.3 %shard_map.100.x_ref.rho_ref = f32[32,24,256]{2,1,0:T(8,128)S(1)} custom-call(f32[32,8,128]{2,1,0:T(8,128)S(1)} %copy-done, s32[32,8,128]{2,1,0:T(8,128)S(1)} %copy-done.2, s32[1]{0:T(128)S(6)} %copy.12.rung_ref, f32[8]{0:T(128)S(1)} %copy-done.4), custom_call_target="tpu_custom_call" | custom-call | flops 5000000000 | bytes 30000000 | tf_op jit(solution)/shard_map/pallas_call | solution.py:448
  15.5 0.0 copy-done.1
  15.5 0.0 copy-done.3
  15.5 0.0 copy-done.6
  15.5 0.0 copy-done.7
  15.5 0.0 copy-done.8
  15.5 0.0 copy-done.9
  15.5 0.0 copy-done.10
  15.6 11.3 %shard_map.101 = (f32[32,8,128]{2,1,0:T(8,128)S(1)}, f32[32,80,256]{2,1,0:T(8,128)S(1)}) custom-call(f32[32,24,256]{2,1,0:T(8,128)S(1)} %shard_map.100.x_ref.rho_ref, f32[32,8,128]{2,1,0:T(8,128)S(1)} %copy-done.1, s32[32,8,128]{2,1,0:T(8,128)S(1)} %copy-done.3, bf16[256,2048]{1,0:T(8,128)(2,1)S(1)} %copy-done.6, bf16[240,240]{1,0:T(8,128)(2,1)S(1)} %copy-done.9, ...), custom_call_target="tpu_custom_call" | custom-call | flops 5000000000 | bytes 30000000 | tf_op jit(solution)/shard_map/pallas_call | solution.py:457
  26.8 0.0 copy-start.5
  26.8 13.2 %shard_map.102 = (f32[32,24,256]{2,1,0:T(8,128)S(1)}, f32[8,128]{1,0:T(8,128)S(1)}) custom-call(f32[32,8,128]{2,1,0:T(8,128)S(1)} %get-tuple-element.9.weight_ref), custom_call_target="tpu_custom_call" | custom-call | flops 5000000000 | bytes 30000000 | tf_op jit(solution)/shard_map/pallas_call | solution.py:466
  40.1 0.0 copy-done.5
  40.1 12.2 %shard_map.103.grad_ref = f32[32,8,128]{2,1,0:T(8,128)S(1)} custom-call(f32[32,24,256]{2,1,0:T(8,128)S(1)} %get-tuple-element.10.x_ref, f32[32,80,256]{2,1,0:T(8,128)S(1)} %get-tuple-element.11.dens_ref, f32[32,24,256]{2,1,0:T(8,128)S(1)} %shard_map.100.x_ref.rho_ref, f32[8,128]{1,0:T(8,128)S(1)} %get-tuple-element.12.sum_ref, s32[1]{0:T(128)S(6)} %copy.12.rung_ref, ...), custom_call_target="tpu_custom_call" | custom-call | flops 5000000000 | bytes 30000000 | tf_op jit(solution)/shard_map/pallas_call | solution.py:478
  52.2 5.8 %shard_map.104 = f32[32,8,128]{2,1,0:T(8,128)S(1)} custom-call(f32[32,8,128]{2,1,0:T(8,128)S(1)} %shard_map.103.grad_ref), custom_call_target="tpu_custom_call" | custom-call | flops 5000000000 | bytes 30000000 | tf_op jit(solution)/shard_map/pallas_call | solution.py:487
  58.1 0.7 %copy.13 = f32[32,8,128]{2,1,0:T(8,128)} copy(f32[32,8,128]{2,1,0:T(8,128)S(1)} %shard_map.104) | data formatting | bytes 262144
Async XLA Ops:
  0.7 0.9 %copy-start = (f32[32,8,128]{2,1,0:T(8,128)S(1)}, f32[32,8,128]{2,1,0:T(8,128)}, u32[]{:S(2)}) copy-start(f32[32,8,128]{2,1,0:T(8,128)} %pot_ref.3) | copy-start | bytes 393220
  1.6 0.9 %copy-start.2 = (s32[32,8,128]{2,1,0:T(8,128)S(1)}, s32[32,8,128]{2,1,0:T(8,128)}, u32[]{:S(2)}) copy-start(s32[32,8,128]{2,1,0:T(8,128)} %lab_ref.3) | copy-start | bytes 393220
  2.5 0.7 %copy-start.4 = (f32[8]{0:T(128)S(1)}, f32[8]{0:T(128)}, u32[]{:S(2)}) copy-start(f32[8]{0:T(128)} %table_ref.2) | copy-start | bytes 100
  3.1 12.4 %copy-start.1 = (f32[32,8,128]{2,1,0:T(8,128)S(1)}, f32[32,8,128]{2,1,0:T(8,128)}, u32[]{:S(2)}) copy-start(f32[32,8,128]{2,1,0:T(8,128)} %pot_ref.3) | copy-start | bytes 393220
  3.1 12.4 %copy-start.3 = (s32[32,8,128]{2,1,0:T(8,128)S(1)}, s32[32,8,128]{2,1,0:T(8,128)}, u32[]{:S(2)}) copy-start(s32[32,8,128]{2,1,0:T(8,128)} %lab_ref.3) | copy-start | bytes 393220
  3.1 12.4 %copy-start.6 = (bf16[256,2048]{1,0:T(8,128)(2,1)S(1)}, bf16[256,2048]{1,0:T(8,128)(2,1)}, u32[]{:S(2)}) copy-start(bf16[256,2048]{1,0:T(8,128)(2,1)} %constant.10.clone.cols_ref) | copy-start | bytes 3145732
  3.1 12.4 %copy-start.7 = (bf16[2304,128]{1,0:T(8,128)(2,1)S(1)}, bf16[2304,128]{1,0:T(8,128)(2,1)}, u32[]{:S(2)}) copy-start(bf16[2304,128]{1,0:T(8,128)(2,1)} %constant.14.clone.colsb_ref) | copy-start | bytes 1769476
  3.1 12.4 %copy-start.8 = (bf16[504,160]{1,0:T(8,128)(2,1)S(1)}, bf16[504,160]{1,0:T(8,128)(2,1)}, u32[]{:S(2)}) copy-start(bf16[504,160]{1,0:T(8,128)(2,1)} %constant.13.clone.back_ref) | copy-start | bytes 483844
  3.1 12.4 %copy-start.9 = (bf16[240,240]{1,0:T(8,128)(2,1)S(1)}, bf16[240,240]{1,0:T(8,128)(2,1)}, u32[]{:S(2)}) copy-start(bf16[240,240]{1,0:T(8,128)(2,1)} %constant.11.clone.box_ref) | copy-start | bytes 345604
  3.2 12.4 %copy-start.10 = (bf16[80,192]{1,0:T(8,128)(2,1)S(1)}, bf16[80,192]{1,0:T(8,128)(2,1)}, u32[]{:S(2)}) copy-start(bf16[80,192]{1,0:T(8,128)(2,1)} %constant.12.clone.mom_ref) | copy-start | bytes 92164
  26.8 13.3 %copy-start.5 = (f32[8]{0:T(128)S(1)}, f32[8]{0:T(128)}, u32[]{:S(2)}) copy-start(f32[8]{0:T(128)} %table_ref.3) | copy-start | bytes 100
